TPU v7x, 256 devices: a whole 4x4x8 slice. The times are simulated.
256 devices in a mesh: segment: 8 (over y, core), fsdp: 32 (over z, x).
Axes of the slice: x: 4, y: 4, z: 8, core: 2. Of those that a mesh axis runs over, the one named last changes fastest.
Arguments:
- tokens: bfloat16 [1024, 6144], P('segment', 'fsdp'), may hold values from -6 to 6
- router_logits: float32 [1024, 2], P('segment'), may hold values from -6 to 6
- routes: int32 [1024, 2], P('segment'), may hold values from 0 to 7, as said below
- loss_weights: int32 [1024], P('segment'), may hold values from 1024 to 8192
- cotangent: bfloat16 [1024, 6144], P('segment', 'fsdp'), may hold values from -6 to 6
- gate_weight: bfloat16 [8, 6144, 8192], P('segment', None, 'fsdp'), may hold values from -0.078125 to 0.078125
- up_weight: bfloat16 [8, 6144, 8192], P('segment', None, 'fsdp'), may hold values from -0.078125 to 0.078125
- down_weight: bfloat16 [8, 8192, 6144], P('segment', 'fsdp'), may hold values from -0.0625 to 0.0625
Outputs:
- output: bfloat16 [1024, 6144], P('segment', 'fsdp')
- input_grad: bfloat16 [1024, 6144], P('segment', 'fsdp')
- down_grad: bfloat16 [8, 8192, 6144], P('segment', 'fsdp')
Inputs may be any that keep to these rules, and one draw needn't show every extreme that they name: `routes`: each row names two different experts. Among the 128 tokens of one index of segment no expert is named more than 64 times, and one expert, the same for every index, is named exactly 64 times by those tokens.
All inputs are finite; a program needn't handle non-finite values.
Results may differ from a plain program's by a relative error of at most 0.035.
Values may be sent and summed in bfloat16 or wider, within the bound.
A program may use at most 128 MiB of HBM per device.

v0:
```python
import jax
import jax.numpy as jnp
from jax import lax
from jax.sharding import PartitionSpec as P


def expert_forward(rows, gate_part, up_part, down_part):
    gate = jnp.dot(rows, gate_part, preferred_element_type=jnp.float32)
    upward = jnp.dot(rows, up_part, preferred_element_type=jnp.float32)
    sigma = jax.nn.sigmoid(gate)
    active = gate * sigma
    hidden = (active * upward).astype(jnp.bfloat16)
    partial_out = jnp.dot(hidden, down_part, preferred_element_type=jnp.float32)
    return (partial_out, (gate, upward, sigma, active, hidden))


def expert_backward(grads, saved, gate_part, up_part, down_part):
    gate, upward, sigma, active, hidden = saved
    contract_last = (((1,), (1,)), ((), ()))
    contract_first = (((0,), (0,)), ((), ()))
    hidden_grad = lax.dot_general(
        grads, down_part, contract_last, preferred_element_type=jnp.float32
    )
    gate_grad = (hidden_grad * upward * (sigma * (1.0 + gate * (1.0 - sigma)))).astype(jnp.bfloat16)
    up_grad = (hidden_grad * active).astype(jnp.bfloat16)
    partial_in = lax.dot_general(
        gate_grad, gate_part, contract_last, preferred_element_type=jnp.float32
    ) + lax.dot_general(up_grad, up_part, contract_last, preferred_element_type=jnp.float32)
    down_grad = lax.dot_general(
        hidden, grads, contract_first, preferred_element_type=jnp.float32
    ).astype(jnp.bfloat16)
    return (partial_in, down_grad)


def expert_rows(buffer, local, capacity):
    sources = buffer.shape[0]
    width = buffer.shape[-1]
    return buffer.reshape(sources, -1, capacity, width)[:, local].reshape(sources * capacity, width)


def section_layout(pieces, sources, capacity):
    stacked = jnp.stack(
        [piece.reshape(sources, capacity, piece.shape[-1]) for piece in pieces], axis=1
    )
    return stacked.reshape(sources, len(pieces) * capacity, stacked.shape[-1])


def build_sends(placing, rows, cotangent, combine, weight_scale, segments):
    pair_count = rows.shape[0] * 2
    width = rows.shape[1]
    scaled = cotangent.astype(jnp.float32) * weight_scale
    pair_grads = (
        (combine[:, :, None] * scaled[:, None, :]).astype(jnp.bfloat16).reshape(pair_count, width)
    )
    pair_tokens = jnp.repeat(rows, 2, axis=0)
    send_rows = (
        jnp.dot(placing, pair_tokens, preferred_element_type=jnp.float32)
        .astype(jnp.bfloat16)
        .reshape(segments, -1, width)
    )
    send_grads = (
        jnp.dot(placing, pair_grads, preferred_element_type=jnp.float32)
        .astype(jnp.bfloat16)
        .reshape(segments, -1, width)
    )
    return (send_rows, send_grads)


def per_device(
    tokens, router_logits, routes, loss_weights, cotangent, gate_weight, up_weight, down_weight
):
    segments = lax.axis_size("segment")
    tok_count = tokens.shape[0]
    share_width = tokens.shape[1]
    local_count = gate_weight.shape[0]
    capacity = tok_count // 2
    expert_count = local_count * segments
    flat_routes = routes.reshape(-1)
    pair_count = flat_routes.shape[0]
    position = jnp.arange(pair_count, dtype=jnp.int32)
    earlier = (flat_routes[:, None] == flat_routes[None, :]) & (
        position[None, :] < position[:, None]
    )
    ranking = jnp.sum(earlier.astype(jnp.int32), axis=1)
    slot_ids = flat_routes * capacity + ranking
    slot_range = jnp.arange(expert_count * capacity, dtype=jnp.int32)
    placing = (slot_range[:, None] == slot_ids[None, :]).astype(jnp.bfloat16)
    share = jax.nn.sigmoid(router_logits[:, 0] - router_logits[:, 1])
    combine = jnp.stack([share, 1.0 - share], axis=1)
    weight_scale = (loss_weights.astype(jnp.float32) / 4096.0)[:, None]
    send_rows, send_grads = build_sends(placing, tokens, cotangent, combine, weight_scale, segments)
    came_rows, came_grads = (
        lax.all_to_all(send_rows, "segment", split_axis=0, concat_axis=0, tiled=True),
        lax.all_to_all(send_grads, "segment", split_axis=0, concat_axis=0, tiled=True),
    )
    section_rows, section_grads = (
        lax.all_gather(came_rows, "fsdp", axis=2, tiled=True),
        lax.all_gather(came_grads, "fsdp", axis=2, tiled=True),
    )
    sources = section_rows.shape[0]
    partial_out, saved = expert_forward(
        expert_rows(section_rows, 0, capacity), gate_weight[0], up_weight[0], down_weight[0]
    )
    partial_in, part_grad = expert_backward(
        expert_rows(section_grads, 0, capacity), saved, gate_weight[0], up_weight[0], down_weight[0]
    )
    outputs = [partial_out]
    inputs = [partial_in]
    weight_grads = [part_grad]
    out_sum, in_sum = (
        lax.psum_scatter(
            section_layout(outputs, sources, capacity).astype(jnp.bfloat16),
            "fsdp",
            scatter_dimension=2,
            tiled=True,
        ).astype(jnp.float32),
        lax.psum_scatter(
            section_layout(inputs, sources, capacity).astype(jnp.bfloat16),
            "fsdp",
            scatter_dimension=2,
            tiled=True,
        ).astype(jnp.float32),
    )
    down_grad = jnp.stack(weight_grads, axis=0)
    back_out, back_in = (
        lax.all_to_all(
            out_sum.astype(jnp.bfloat16), "segment", split_axis=0, concat_axis=0, tiled=True
        ),
        lax.all_to_all(
            in_sum.astype(jnp.bfloat16), "segment", split_axis=0, concat_axis=0, tiled=True
        ),
    )
    contract_first = (((0,), (0,)), ((), ()))
    picked_out = lax.dot_general(
        placing,
        back_out.reshape(-1, share_width),
        contract_first,
        preferred_element_type=jnp.float32,
    ).reshape(tok_count, 2, share_width)
    picked_in = lax.dot_general(
        placing,
        back_in.reshape(-1, share_width),
        contract_first,
        preferred_element_type=jnp.float32,
    ).reshape(tok_count, 2, share_width)
    output = (combine[:, 0:1] * picked_out[:, 0] + combine[:, 1:2] * picked_out[:, 1]).astype(
        jnp.bfloat16
    )
    input_grad = (picked_in[:, 0] + picked_in[:, 1]).astype(jnp.bfloat16)
    return (output, input_grad, down_grad)


def solution(mesh):
    in_specs = (
        P("segment", "fsdp"),
        P("segment", None),
        P("segment", None),
        P("segment"),
        P("segment", "fsdp"),
        P("segment", None, "fsdp"),
        P("segment", None, "fsdp"),
        P("segment", "fsdp", None),
    )
    out_specs = (P("segment", "fsdp"), P("segment", "fsdp"), P("segment", "fsdp", None))
    return jax.shard_map(
        per_device, mesh=mesh, in_specs=in_specs, out_specs=out_specs, check_vma=False
    )
```

profile of v0, /device:TPU:8, one launch (start us, length us, event | category | flops | bytes accessed | tf_op | source)
XLA Modules:
  0.0 741.7 jit_solution(14815749613790866720)
XLA Ops:
  7.2 0.0 copy-start
  7.2 0.0 all-gather.3.cloned.1.call-start
  7.2 1.0 copy.54
  8.3 0.1 broadcast_in_dim.2
  8.4 0.1 reshape.86
  8.5 0.8 copy.53
  9.3 0.1 reshape.85
  9.4 0.2 convert_reduce_fusion
  9.6 1.0 convolution_convert_fusion.3
  10.6 1.1 copy.55
  11.6 11.3 %all_to_all.20 = bf16[8,64,192]{2,1,0:T(8,128)(2,1)} all-to-all(bf16[8,64,192]{2,1,0:T(8,128)(2,1)S(1)} %bitcast.76), channel_id=1, replica_groups=mesh['segment'=8,'fsdp'=32] {'segment'}, dimensions={0} | all-to-all | bytes 393216 | tf_op jit(solution)/shard_map/all_to_all | solution.py:93
  23.0 1.9 copy.56
  24.9 0.0 all-gather.3.cloned.1.call-update
  24.9 0.0 all-gather.5.cloned.1.call-start
  25.0 0.8 broadcast_subtract_fusion
  25.8 0.1 copy.60
  25.9 0.1 mul.87
  26.0 0.7 convert_multiply_fusion.1
  26.7 0.8 convert_multiply_fusion
  27.5 0.1 copy.61
  27.6 0.8 mul.91
  28.4 1.1 mul.92
  29.5 1.0 convolution_convert_fusion.2
  30.5 1.1 copy.62
  31.6 10.6 %all_to_all.21 = bf16[8,64,192]{2,1,0:T(8,128)(2,1)} all-to-all(bf16[8,64,192]{2,1,0:T(8,128)(2,1)S(1)} %bitcast.77), channel_id=1, replica_groups=mesh['segment'=8,'fsdp'=32] {'segment'}, dimensions={0} | all-to-all | bytes 393216 | tf_op jit(solution)/shard_map/all_to_all | solution.py:94
  42.2 1.9 copy.63
  44.1 0.0 all-gather.5.cloned.1.call-update
  44.1 0.0 reduce-scatter.7.cloned.1.call-start
  44.2 102.0 %all-gather.3.cloned.1.call-done = bf16[8,64,6144]{1,0,2:T(8,128)(2,1)} async-done(((bf16[8,64,192]{1,0,2:T(8,128)(2,1)}), bf16[8,64,6144]{1,0,2:T(8,128)(2,1)}) %all-gather.3.cloned.1.call-update) | async-done | bytes 6291472 | tf_op jit(solution)/shard_map/all_gather | solution.py:97
  146.1 14.1 %copy.57 = bf16[8,64,6144]{2,1,0:T(8,128)(2,1)} copy(bf16[8,64,6144]{1,0,2:T(8,128)(2,1)} %all-gather.3.cloned.1.call-done) | data formatting | bytes 12582912 | tf_op jit(solution)/shard_map/all_gather | solution.py:97
  160.2 5.6 fusion.9
  165.9 0.0 copy-done
  165.9 0.0 copy-start.1
  166.0 2.6 multiply_convert_fusion.2
  168.6 4.5 convolution_convert_fusion
  173.1 14.5 %copy.71 = bf16[8,64,6144]{1,0,2:T(8,128)(2,1)} copy(bf16[8,64,6144]{2,1,0:T(8,128)(2,1)} %convolution_convert_fusion) | data formatting | bytes 12582912
  187.6 17.2 %reshape.94 = bf16[6144,512]{1,0:T(8,128)(2,1)} reshape(bf16[6144,8,64]{2,1,0:T(8,128)(2,1)} %bitcast.64) | data formatting | bytes 12582912
  204.8 0.0 reduce-scatter.7.cloned.1.call-update
  204.8 0.2 reduce-scatter.9.cloned.1.call-start
  205.1 60.4 %all-gather.5.cloned.1.call-done = bf16[8,64,6144]{1,0,2:T(8,128)(2,1)} async-done(((bf16[8,64,192]{1,0,2:T(8,128)(2,1)}), bf16[8,64,6144]{1,0,2:T(8,128)(2,1)}) %all-gather.5.cloned.1.call-update) | async-done | bytes 6291472 | tf_op jit(solution)/shard_map/all_gather | solution.py:98
  265.5 14.0 %copy.64 = bf16[8,64,6144]{2,1,0:T(8,128)(2,1)} copy(bf16[8,64,6144]{1,0,2:T(8,128)(2,1)} %all-gather.5.cloned.1.call-done) | data formatting | bytes 12582912 | tf_op jit(solution)/shard_map/all_gather | solution.py:98
  279.5 5.7 fusion.2
  285.2 6.5 fusion.7
  291.7 9.1 %add_convert_fusion = bf16[512,6144]{1,0:T(8,128)(2,1)} fusion(f32[512,6144]{1,0:T(8,128)} %fusion.7, bf16[1,6144,256]{2,1,0:T(8,128)(2,1)S(1)} %copy-done, f32[512,256]{1,0:T(8,128)S(1)} %fusion.2, f32[512,256]{1,0:T(8,128)S(1)} %copy-done.4), kind=kOutput, calls=%fused_computation | convolution fusion | flops 1617690624 | bytes 23068672 | tf_op jit(solution)/shard_map/dot_general | solution.py:28
  300.8 14.5 %copy.73 = bf16[8,64,6144]{1,0,2:T(8,128)(2,1)} copy(bf16[8,64,6144]{2,1,0:T(8,128)(2,1)} %bitcast.68) | data formatting | bytes 12582912
  315.3 17.2 %reshape.96 = bf16[6144,512]{1,0:T(8,128)(2,1)} reshape(bf16[6144,8,64]{2,1,0:T(8,128)(2,1)} %bitcast.65) | data formatting | bytes 12582912
  332.5 0.0 reduce-scatter.9.cloned.1.call-update
  332.5 0.1 iota_compare_fusion.3
  332.7 0.8 eq.50
  333.5 157.9 %reduce-scatter.7.cloned.1.call-done = bf16[192,512]{1,0:T(8,128)(2,1)} async-done(((bf16[6144,512]{1,0:T(8,128)(2,1)}), bf16[192,512]{1,0:T(8,128)(2,1)}) %reduce-scatter.7.cloned.1.call-update) | async-done | bytes 196624
  491.4 1.9 reshape.95
  493.3 1.9 copy.72
  495.2 4.9 all-to-all-start.1
  500.1 6.3 fusion
  506.4 212.3 %reduce-scatter.9.cloned.1.call-done = bf16[192,512]{1,0:T(8,128)(2,1)} async-done(((bf16[6144,512]{1,0:T(8,128)(2,1)}), bf16[192,512]{1,0:T(8,128)(2,1)}) %reduce-scatter.9.cloned.1.call-update) | async-done | bytes 196624
  718.7 1.2 reshape.97
  719.8 1.0 copy.74
  720.8 0.0 all-to-all-done.1
  720.8 4.8 all-to-all-start.3
  725.6 2.0 fusion.18
  727.6 4.1 all-to-all-done.3
  731.7 1.2 fusion.16
  732.9 0.6 fusion.27
  733.6 1.6 fusion.24
  (17 shorter events, 0.0 us)
Async XLA Ops:
  7.2 158.7 %copy-start = (bf16[1,6144,256]{2,1,0:T(8,128)(2,1)S(1)}, bf16[1,6144,256]{2,1,0:T(8,128)(2,1)}, u32[]{:S(2)}) copy-start(bf16[1,6144,256]{2,1,0:T(8,128)(2,1)} %param.14) | copy-start | bytes 9437188
  7.2 139.0 %all-gather.3.cloned.1.call-start = ((), (), s32[]{:S(2)}) async-start(), calls=%async_computation.6 | async-start | bytes 12976128 | tf_op jit(solution)/shard_map/all_gather | solution.py:97
  24.9 240.6 %all-gather.5.cloned.1.call-start = ((), (), s32[]{:S(2)}) async-start(), calls=%async_computation.7 | async-start | bytes 12976128 | tf_op jit(solution)/shard_map/all_gather | solution.py:98
  44.1 447.3 %reduce-scatter.7.cloned.1.call-start = ((), (), s32[]{:S(2)}) async-start(), calls=%async_computation.8 | async-start | bytes 6488064
  160.2 5.7 slice-start
  160.2 5.7 slice-start.1
  165.9 2.6 copy-start.3
  165.9 2.6 copy-start.1
  204.8 513.8 %reduce-scatter.9.cloned.1.call-start = ((), (), s32[]{:S(2)}) async-start(), calls=%async_computation.9 | async-start | bytes 6488064
  279.5 5.7 copy-start.2
  279.5 5.7 copy-start.4
  279.5 5.7 copy-start.5
  495.2 225.6 %all-to-all-start.1 = ((bf16[8,64,192]{2,1,0:T(8,128)(2,1)}), bf16[8,64,192]{2,1,0:T(8,128)(2,1)}, u32[]{:S(2)}, u32[]{:S(2)}) async-start(bf16[8,64,192]{2,1,0:T(8,128)(2,1)} %copy.72), calls=%async_computation.1 | async-start | bytes 524288 | tf_op jit(solution)/shard_map/all_to_all | solution.py:126
  720.8 10.9 %all-to-all-start.3 = ((bf16[8,64,192]{2,1,0:T(8,128)(2,1)}), bf16[8,64,192]{2,1,0:T(8,128)(2,1)S(1)}, u32[]{:S(2)}, u32[]{:S(2)}) async-start(bf16[8,64,192]{2,1,0:T(8,128)(2,1)} %copy.74), calls=%async_computation.3 | async-start | bytes 524288 | tf_op jit(solution)/shard_map/all_to_all | solution.py:129
Sparse Core Ops, SparseCore 0:
  25.0 121.0 all-gather.2
  148.7 116.7 all-gather.4
  269.5 221.8 reduce-scatter.6
  495.8 222.8 reduce-scatter.8
where the time goes:
time: 746 us; the launch traced here: 742 us
  waiting for transfers between devices  537 us (72%)
  local copies, waits for them, and re-layouts  109 us (15%)
  matrix products  45.5 us (6%)
  blocking collectives  21.9 us (3%)
  between operations  14 us (2%)
  starting transfers between devices  10 us (1%)
    unnamed x6, waiting for transfers between devices  370 us
    all_gather x1, waiting for transfers between devices, per_device(): lax.all_gather(came_rows, 'fsdp', axis=2, tiled=True)  102 us
    unnamed x26, local copies, waits for them, and re-layouts  71.2 us
    all_gather x1, waiting for transfers between devices, per_device(): lax.all_gather(came_grads, 'fsdp', axis=2, tiled=True)  60.4 us
  transfers between devices with their start and end apart: 6, of which 5 were waited for; matrix products, arithmetic and copies ran while one was open for 20% of the time, Pallas kernels for 0%

commit v1 on v0

v1 whole, which is shorter than its diff:
```python
import functools

import jax
import jax.numpy as jnp
from jax import lax
from jax.experimental import pallas as pl
from jax.experimental.pallas import tpu as pltpu
from jax.sharding import PartitionSpec as P

MESH = pl.DeviceIdType.MESH
BF = jnp.bfloat16
F32 = jnp.float32
NX, NY, NZ = 4, 4, 8
FEAT, TOK = 64, 128


def dot(a, b):
    return lax.dot_general(a, b, (((1,), (0,)), ((), ())), preferred_element_type=F32)


def dot_nt(a, b):
    return lax.dot_general(a, b, (((1,), (1,)), ((), ())), preferred_element_type=F32)


class Place:
    def __init__(self):
        seg, fsdp = lax.axis_index("segment"), lax.axis_index("fsdp")
        self.seg = seg
        self.y, self.c = seg // 2, seg % 2
        self.z, self.x = fsdp // NX, fsdp % NX

    def at(self, dx=0, dy=0, dz=0, sibling=False):
        x = (self.x + dx) % NX
        y = (self.y + dy) % NY
        z = (self.z + dz) % NZ
        c = 1 - self.c if sibling else self.c
        return (y * 2 + c, z * NX + x)

    def others(self):
        found = [self.at(sibling=True)]
        found += [self.at(dx=d) for d in range(1, NX)]
        found += [self.at(dy=d) for d in range(1, NY)]
        found += [self.at(dz=d) for d in range(1, NZ)]
        return found


def enter(devices):
    barrier = pltpu.get_barrier_semaphore()
    for device in devices:
        pl.semaphore_signal(barrier, inc=1, device_id=device, device_id_type=MESH)
    return lambda: pl.semaphore_wait(barrier, len(devices))


def a_base(y, z, half):
    return z * 4 + 2 * half


def brick_of(bases, t):
    base = bases[0]
    for k in range(1, len(bases)):
        base = jnp.where(t // 2 == k, bases[k], base)
    return base + t % 2


def weight_of(b):
    in_b = 8 + ((b - 32) // 8) * 2 + b % 2
    in_c = 16 + (((b - 64) // 2) % 4) * 2 + b % 2
    return jnp.where(b < 32, b // 4, jnp.where(b < 64, in_b, in_c))


def row_of(b):
    return jnp.where(b < 32, b % 4, jnp.where(b < 64, ((b - 32) // 2) % 4, (b - 64) // 8))


def mult(value, of):
    return pl.multiple_of(value, of)


class Copies:
    def __init__(self, send, recv):
        self.send, self.recv = send, recv
        self.index = {}
        self.sent = []

    def number(self, key):
        return self.index.setdefault(key, len(self.index))

    def make(self, key, src, dst, device):
        i = self.number(key)
        return pltpu.make_async_remote_copy(
            src_ref=src,
            dst_ref=dst,
            send_sem=self.send.at[i],
            recv_sem=self.recv.at[i],
            device_id=device,
            device_id_type=MESH,
        )

    def start(self, key, src, dst, device):
        copy = self.make(key, src, dst, device)
        copy.start()
        self.sent.append(copy)

    def arrived(self, key, ref, device):
        self.make(key, ref, ref, device).wait_recv()

    def drain(self):
        for copy in self.sent:
            copy.wait_send()


class Gather:
    def __init__(self, name, place, copies, buf):
        self.name, self.at, self.copies, self.buf = name, place, copies, buf

    def key(self, *rest):
        return (self.name,) + rest

    def atoms(self, x, z):
        p = self.at
        low = mult((z % 4) * FEAT, FEAT)
        return (
            self.buf.at[p.c, z * 4 + p.y, pl.ds(mult(x * FEAT, FEAT), FEAT)],
            self.buf.at[p.c, 32 + (x * 4 + p.y) * 2 + z // 4, pl.ds(low, FEAT)],
            self.buf.at[p.c, 64 + (p.y * 4 + x) * 2 + z // 4, pl.ds(low, FEAT)],
        )

    def put_own(self, block_t):
        p = self.at
        low = mult((p.z % 4) * FEAT, FEAT)
        self.buf[p.c, p.z * 4 + p.y, pl.ds(mult(p.x * FEAT, FEAT), FEAT), :] = block_t[0:64]
        self.buf[p.c, 32 + (p.x * 4 + p.y) * 2 + p.z // 4, pl.ds(low, FEAT), :] = block_t[64:128]
        self.buf[p.c, 64 + (p.y * 4 + p.x) * 2 + p.z // 4, pl.ds(low, FEAT), :] = block_t[128:192]

    def send_first(self):
        p = self.at
        a, b, c = self.atoms(p.x, p.z)
        for d in range(1, NX):
            self.copies.start(self.key("a1", d), a, a, p.at(dx=d))
        for d in range(1, NZ):
            self.copies.start(self.key("b1", d), b, b, p.at(dz=d))
            self.copies.start(self.key("c1", d), c, c, p.at(dz=d))

    def wait_first_a(self):
        p = self.at
        for d in range(1, NX):
            a, _, _ = self.atoms((p.x - d) % NX, p.z)
            self.copies.arrived(self.key("a1", d), a, p.at(dx=-d))

    def wait_first_bc(self):
        p = self.at
        for d in range(1, NZ):
            _, b, c = self.atoms(p.x, (p.z - d) % NZ)
            self.copies.arrived(self.key("b1", d), b, p.at(dz=-d))
            self.copies.arrived(self.key("c1", d), c, p.at(dz=-d))

    def second(self, part, d):
        p = self.at
        if part == "a":
            return self.buf.at[p.c, pl.ds(p.z * 4 + (p.y - d) % NY, 1)], p.at(dy=-d)
        if part == "b":
            return self.buf.at[p.c, pl.ds(32 + (p.x * 4 + (p.y - d) % NY) * 2, 2)], p.at(dy=-d)
        return self.buf.at[p.c, pl.ds(64 + (p.y * 4 + (p.x - d) % NX) * 2, 2)], p.at(dx=-d)

    def send_second(self, part):
        p = self.at
        block, _ = self.second(part, 0)
        for d in range(1, 4):
            device = p.at(dx=d) if part == "c" else p.at(dy=d)
            self.copies.start(self.key(part + "2", d), block, block, device)

    def wait_second(self, part):
        for d in range(1, 4):
            block, device = self.second(part, d)
            self.copies.arrived(self.key(part + "2", d), block, device)

    def chunk(self, base):
        return self.buf.at[self.at.c, pl.ds(base, 2)]

    def neighbour(self, part, sign):
        p = self.at
        return {"a": p.at(dz=sign), "b": p.at(dx=sign), "c": p.at(dy=sign)}[part]

    def base(self, part, sign, m):
        p = self.at
        if part == "a":
            z = (p.z - sign * (1 + m // 2)) % NZ
            half = m % 2 if sign > 0 else 1 - m % 2
            return z * 4 + 2 * half
        hop = 1 if m < 4 else 2
        q = m % 4 if sign > 0 else (m + 2) % 4
        if part == "b":
            return 32 + (((p.x - sign * hop) % NX) * 4 + q) * 2
        return 64 + (((p.y - sign * hop) % NY) * 4 + q) * 2

    def own_base(self, part, sign, m):
        p = self.at
        if part == "a":
            return p.z * 4 + 2 * (m % 2 if sign > 0 else 1 - m % 2)
        q = m % 4 if sign > 0 else (m + 2) % 4
        if part == "b":
            return 32 + (p.x * 4 + q) * 2
        return 64 + (p.y * 4 + q) * 2

    def own_span(self, part):
        p = self.at
        if part == "a":
            return self.buf.at[p.c, pl.ds(p.z * 4, 4)]
        if part == "b":
            return self.buf.at[p.c, pl.ds(32 + p.x * 8, 8)]
        return self.buf.at[p.c, pl.ds(64 + p.y * 8, 8)]

    def other_span(self, part):
        p = self.at
        if part == "a":
            return self.buf.at[1 - p.c, pl.ds(p.z * 4, 4)]
        if part == "b":
            return self.buf.at[1 - p.c, pl.ds(32 + p.x * 8, 8)]
        return self.buf.at[1 - p.c, pl.ds(64 + p.y * 8, 8)]

    def start_ring(self, part):
        for m in range(2 if part == "a" else 4):
            for sign in (1, -1):
                ref = self.chunk(self.own_base(part, sign, m))
                self.copies.start(self.key(part, sign, m), ref, ref, self.neighbour(part, sign))
        ref = self.own_span(part)
        self.copies.start(self.key("own", part), ref, ref, self.at.at(sibling=True))

    def messages(self, m):
        return [
            (part, sign)
            for part in ("a", "b", "c")
            if m < (7 if part == "a" else 6)
            for sign in (1, -1)
        ]

    def bases(self, m):
        return [self.base(part, sign, m) for part, sign in self.messages(m)]

    def ring_round(self, m):
        for part, sign in self.messages(m):
            ref = self.chunk(self.base(part, sign, m))
            self.copies.arrived(self.key(part, sign, m), ref, self.neighbour(part, -sign))
            step = 2 if part == "a" else 4
            if m + step < (7 if part == "a" else 6):
                self.copies.start(
                    self.key(part, sign, m + step), ref, ref, self.neighbour(part, sign)
                )
            self.copies.start(self.key("sib", part, sign, m), ref, ref, self.at.at(sibling=True))

    def wait_other(self, m):
        p = self.at
        for part, sign in self.messages(m):
            ref = self.buf.at[1 - p.c, pl.ds(self.base(part, sign, m), 2)]
            self.copies.arrived(self.key("sib", part, sign, m), ref, p.at(sibling=True))

    def wait_other_own(self):
        for part in ("a", "b", "c"):
            self.copies.arrived(
                self.key("own", part), self.other_span(part), self.at.at(sibling=True)
            )

    def multiply(self, weights, total, bricks, count):
        def step(t, carry):
            b = bricks(t)
            row = row_of(b)
            rhs = jnp.concatenate([self.buf[0, b], self.buf[1, b]], axis=1)
            total[row] += dot(weights(weight_of(b)), rhs)
            return carry

        lax.fori_loop(0, count, step, 0)

    def multiply_own(self, weights, total):
        p = self.at

        def bricks(t):
            return jnp.where(
                t < 4,
                p.z * 4 + t,
                jnp.where(t < 12, 32 + p.x * 8 + t - 4, 64 + p.y * 8 + t - 12),
            )

        self.multiply(weights, total, bricks, 20)

    def multiply_round(self, weights, total, m):
        bases = self.bases(m)
        self.multiply(weights, total, lambda t: brick_of(bases, t), 2 * len(bases))


def load_blocks(hbm, part_ref, sem):
    for z in range(NZ):
        pltpu.make_async_copy(hbm.at[z, :, 0], part_ref(z), sem).start()
    for x in range(NX):
        for h in range(2):
            for part, first in ((1, 8), (2, 16)):
                pltpu.make_async_copy(
                    hbm.at[pl.ds(h * 4, 4), x, part], part_ref(first + x * 2 + h), sem
                ).start()


def gather_kernel(
    meta_ref,
    tok_ref,
    cot_ref,
    gate_hbm,
    up_hbm,
    down_hbm,
    hid_ref,
    grads_ref,
    wd_ref,
    dgrad_hbm,
    tok_buf,
    cot_buf,
    wgu,
    wdt,
    flat,
    total,
    hgrad,
    scaled,
    meta,
    wsem,
    osem,
    send,
    recv,
):
    p = Place()
    copies = Copies(send, recv)
    tok = Gather("tok", p, copies, tok_buf)
    cot = Gather("cot", p, copies, cot_buf)
    far = [((p.seg + d) % 8, p.z * NX + p.x) for d in range(1, 8)]
    line = [p.at(dx=d) for d in range(1, NX)] + [p.at(dz=d) for d in range(1, NZ)]
    entered = enter(line + far)

    load_blocks(gate_hbm, lambda w: wgu.at[w, 0], wsem.at[0])
    load_blocks(up_hbm, lambda w: wgu.at[w, 1], wsem.at[0])
    pltpu.make_async_copy(down_hbm, flat, wsem.at[1]).start()

    tok.put_own(tok_ref[...].astype(F32).T.astype(BF))
    cot.put_own(cot_ref[...].astype(F32).T.astype(BF))
    meta[p.seg] = meta_ref[p.seg]
    total[...] = jnp.zeros_like(total)
    hgrad[...] = jnp.zeros_like(hgrad)
    entered()

    tok.send_first()
    for d in range(1, 8):
        copies.start(("meta", d), meta_ref.at[(p.seg + d) % 8], meta.at[p.seg], far[d - 1])

    pltpu.make_async_copy(wgu, wgu, wsem.at[0]).wait()

    def turn_gu(w, carry):
        for k in range(2):
            block = wgu[w, k].reshape(256, 256)
            wgu[w, k] = block.T.reshape(4, 64, 256)
        return carry

    lax.fori_loop(0, 6, turn_gu, 0)
    tok.wait_first_a()
    tok.send_second("a")
    lax.fori_loop(6, 12, turn_gu, 0)
    tok.wait_first_bc()
    tok.send_second("b")
    tok.send_second("c")
    tok.wait_second("a")
    tok.start_ring("a")
    cot.send_first()
    lax.fori_loop(12, 24, turn_gu, 0)
    tok.wait_second("b")
    tok.start_ring("b")
    tok.wait_second("c")
    tok.start_ring("c")
    pltpu.make_async_copy(down_hbm, flat, wsem.at[1]).wait()

    def turn_down(i, carry):
        block = flat[:, pl.ds(mult(i * 384, 384), 384)].T
        z, x = i // 2, (i % 2) * 2
        for k in range(2):
            rows = block[k * 192 : (k + 1) * 192]
            wd_ref[z, x + k] = rows[0:64]
            wd_ref[8 + (x + k) * 2 + z // 4, z % 4] = rows[64:128]
            wd_ref[16 + (x + k) * 2 + z // 4, z % 4] = rows[128:192]
        return carry

    def turn_back(w, carry):
        wdt[w] = wd_ref[w].reshape(256, 256).T
        return carry

    def w_gu(w):
        return wgu[w].reshape(512, 256)

    def w_down(w):
        return wdt[w]

    for m in range(7):
        tok.ring_round(m)
        if m == 0:
            tok.wait_other_own()
            tok.multiply_own(w_gu, total)
        else:
            tok.wait_other(m - 1)
            tok.multiply_round(w_gu, total, m - 1)
        if m == 1:
            cot.wait_first_a()
            cot.send_second("a")
            cot.wait_first_bc()
            cot.send_second("b")
            cot.send_second("c")
            lax.fori_loop(0, 8, turn_down, 0)
        if m == 2:
            lax.fori_loop(8, 16, turn_down, 0)
        if m == 3:
            lax.fori_loop(0, 12, turn_back, 0)
        if m == 4:
            for part in ("a", "b", "c"):
                cot.wait_second(part)
                cot.start_ring(part)
            lax.fori_loop(12, 24, turn_back, 0)
    cot.ring_round(0)
    tok.wait_other(6)
    tok.multiply_round(w_gu, total, 6)
    for d in range(1, 8):
        copies.arrived(("meta", d), meta.at[(p.seg - d) % 8], far[7 - d])

    def activate(i, carry):
        y, r = i // 4, i % 4
        low = mult(r * 64, 64)
        gate = total[y, pl.ds(low, 64)]
        upward = total[y, pl.ds(mult(256 + r * 64, 64), 64)]
        first, second = meta[2 * y], meta[2 * y + 1]
        share = jnp.concatenate([first[0:1], second[0:1]], axis=1)
        scale = jnp.concatenate([first[1:2], second[1:2]], axis=1)
        sigma = jax.nn.sigmoid(gate)
        active = gate * sigma
        hidden = active * upward
        weighted = (hidden * share).astype(BF)
        hid_ref[y, 0, pl.ds(low, 64)] = weighted[:, 0:128]
        hid_ref[y, 1, pl.ds(low, 64)] = weighted[:, 128:256]
        scaled[y, pl.ds(low, 64)] = (hidden * scale).astype(BF)
        total[y, pl.ds(low, 64)] = upward * (sigma * (1.0 + gate * (1.0 - sigma))) * scale
        total[y, pl.ds(mult(256 + r * 64, 64), 64)] = active * scale
        return carry

    lax.fori_loop(0, 16, activate, 0)

    for m in range(7):
        if m > 0:
            cot.ring_round(m)
        if m == 0:
            cot.wait_other_own()
            cot.multiply_own(w_down, hgrad)
        else:
            cot.wait_other(m - 1)
            cot.multiply_round(w_down, hgrad, m - 1)
    cot.wait_other(6)
    cot.multiply_round(w_down, hgrad, 6)

    def backward(i, carry):
        y, r = i // 4, i % 4
        low = mult(r * 64, 64)
        high = mult(256 + r * 64, 64)
        grad = hgrad[y, pl.ds(low, 64)]
        gate_grad = (grad * total[y, pl.ds(low, 64)]).astype(BF)
        up_grad = (grad * total[y, pl.ds(high, 64)]).astype(BF)
        for c in range(2):
            grads_ref[y, c, pl.ds(low, 64)] = gate_grad[:, c * 128 : (c + 1) * 128]
            grads_ref[y, c, pl.ds(high, 64)] = up_grad[:, c * 128 : (c + 1) * 128]
        return carry

    lax.fori_loop(0, 16, backward, 0)

    def weight_grad(i, carry):
        z, x = i // 2, (i % 2) * 2
        low = mult((z % 4) * FEAT, FEAT)
        acc = jnp.zeros((256, 384), F32)
        for y in range(NY):
            halves = []
            for c in range(2):
                rows = []
                for k in range(2):
                    xk = x + k
                    rows.append(cot_buf[c, z * 4 + y, pl.ds(mult(xk * FEAT, FEAT), FEAT), :])
                    rows.append(cot_buf[c, 32 + (xk * 4 + y) * 2 + z // 4, pl.ds(low, FEAT), :])
                    rows.append(cot_buf[c, 64 + (y * 4 + xk) * 2 + z // 4, pl.ds(low, FEAT), :])
                halves.append(jnp.concatenate(rows, axis=0))
            acc += dot_nt(scaled[y], jnp.concatenate(halves, axis=1))
        flat[:, pl.ds(mult(i * 384, 384), 384)] = acc.astype(BF)
        return carry

    lax.fori_loop(0, 16, weight_grad, 0)
    out = pltpu.make_async_copy(flat, dgrad_hbm, osem)
    out.start()
    copies.drain()
    out.wait()


RING = (("a", 1), ("a", -1), ("b", 1), ("b", -1), ("c", 1), ("c", -1))


class Scatter:
    def __init__(self, name, place, copies, lhs, rhs, pairs, ring, stage, bufs):
        self.name, self.at, self.copies = name, place, copies
        self.lhs, self.rhs, self.pairs, self.ring, self.stage = lhs, rhs, pairs, ring, stage
        self.two, self.three_a, self.three_bc, self.sums = bufs

    def key(self, *rest):
        return (self.name,) + rest

    def base(self, part, sign, m):
        p = self.at
        if part == "a":
            hop = 4 - (m + 1) // 2
            half = m % 2 if sign > 0 else 1 - m % 2
            return ((p.z + sign * hop) % NZ) * 4 + 2 * half
        hop = 2 if m < 2 else 1
        q = m % 4 if sign > 0 else (m + 2) % 4
        if part == "b":
            return 32 + (((p.x + sign * hop) % NX) * 4 + q) * 2
        return 64 + (((p.y + sign * hop) % NY) * 4 + q) * 2

    def own(self, part, q):
        p = self.at
        if part == "a":
            return p.z * 4 + 2 * q
        if part == "b":
            return 32 + (p.x * 4 + q) * 2
        return 64 + (p.y * 4 + q) * 2

    def groups(self, j):
        if j < 6:
            return [self.base(part, sign, j) for part, sign in RING]
        if j == 6:
            return [self.base("a", 1, 6), self.base("a", -1, 6)] + [
                self.own(part, q) for part in ("a", "b") for q in range(2)
            ]
        return [self.own("b", 2), self.own("b", 3)] + [self.own("c", q) for q in range(4)]

    def keys(self, j):
        if j < 6:
            return [(part, sign, j) for part, sign in RING]
        if j == 6:
            return [("a", 1, 6), ("a", -1, 6)] + [
                ("own", part, q) for part in ("a", "b") for q in range(2)
            ]
        return [("own", "b", 2), ("own", "b", 3)] + [("own", "c", q) for q in range(4)]

    def product(self, b, c):
        return dot(self.lhs(weight_of(b)), self.rhs(row_of(b), c))

    def hand_over(self, j, slot):
        p = self.at
        bases = self.groups(j)

        def step(t, carry):
            b = brick_of(bases, t)
            self.stage[slot, t] = self.product(b, 1 - p.c).astype(BF)
            return carry

        lax.fori_loop(0, 12, step, 0)
        for k, (key, base) in enumerate(zip(self.keys(j), bases)):
            self.copies.start(
                self.key("sib") + key,
                self.stage.at[slot, pl.ds(2 * k, 2)],
                self.pairs.at[pl.ds(base, 2)],
                p.at(sibling=True),
            )

    def handed(self, key, base):
        self.copies.arrived(
            self.key("sib") + key, self.pairs.at[pl.ds(base, 2)], self.at.at(sibling=True)
        )

    def neighbour(self, part, sign):
        p = self.at
        return {"a": p.at(dz=sign), "b": p.at(dx=sign), "c": p.at(dy=sign)}[part]

    def came(self, k, m):
        part, sign = RING[k]
        self.copies.arrived(
            self.key(part, sign, m), self.ring.at[k, m], self.neighbour(part, -sign)
        )

    def send_round(self, m):
        p = self.at
        for k, (part, sign) in enumerate(RING):
            if m >= (7 if part == "a" else 6):
                continue
            base = self.base(part, sign, m)
            self.handed((part, sign, m), base)
            back = m - (2 if part == "a" else 4)
            if back >= 0:
                self.came(k, back)

            def step(t, carry):
                b = base + t
                value = self.product(b, p.c) + self.pairs[b].astype(F32)
                if back >= 0:
                    value += self.ring[k, back, t].astype(F32)
                self.pairs[b] = value.astype(BF)
                return carry

            lax.fori_loop(0, 2, step, 0)
            self.copies.start(
                self.key(part, sign, m),
                self.pairs.at[pl.ds(base, 2)],
                self.ring.at[k, m],
                self.neighbour(part, sign),
            )

    def finish_ring(self):
        p = self.at
        for part, first, count in (("a", 0, 2), ("b", 2, 4), ("c", 4, 4)):
            for q in range(count):
                base = self.own(part, q)
                self.handed(("own", part, q), base)
                if part == "a":
                    plus, minus = 6 - q, 5 + q
                else:
                    plus, minus = 2 + (q + 2) % 4, 2 + q
                self.came(first, plus)
                self.came(first + 1, minus)

                def step(t, carry):
                    b = base + t
                    value = self.product(b, p.c) + self.pairs[b].astype(F32)
                    value += self.ring[first, plus, t].astype(F32)
                    value += self.ring[first + 1, minus, t].astype(F32)
                    self.pairs[b] = value.astype(BF)
                    return carry

                lax.fori_loop(0, 2, step, 0)

    def second(self, part, d):
        p = self.at
        if part == "a":
            return pl.ds(p.z * 4 + (p.y + d) % NY, 1), pl.ds(0, 1), p.at(dy=d)
        if part == "b":
            return pl.ds(32 + (p.x * 4 + (p.y + d) % NY) * 2, 2), pl.ds(1, 2), p.at(dy=d)
        return pl.ds(64 + (p.y * 4 + (p.x + d) % NX) * 2, 2), pl.ds(3, 2), p.at(dx=d)

    def send_second(self):
        for part in ("a", "b", "c"):
            for d in range(1, 4):
                bricks, slot, device = self.second(part, d)
                self.copies.start(
                    self.key(part + "2", d),
                    self.pairs.at[bricks],
                    self.two.at[d - 1, slot],
                    device,
                )

    def sum_second(self):
        p = self.at
        for part, slots in (("a", (0,)), ("b", (1, 2)), ("c", (3, 4))):
            for d in range(1, 4):
                _, slot, _ = self.second(part, d)
                device = p.at(dx=-d) if part == "c" else p.at(dy=-d)
                self.copies.arrived(self.key(part + "2", d), self.two.at[d - 1, slot], device)
            for t, slot in enumerate(slots):
                mine = {
                    "a": p.z * 4 + p.y,
                    "b": 32 + (p.x * 4 + p.y) * 2 + t,
                    "c": 64 + (p.y * 4 + p.x) * 2 + t,
                }[part]
                value = self.pairs[mine].astype(F32)
                for d in range(3):
                    value += self.two[d, slot].astype(F32)
                self.sums[slot] = value.astype(BF).reshape(4, 64, TOK)
        for d in range(1, NX):
            x = (p.x + d) % NX
            self.copies.start(
                self.key("a3", d), self.sums.at[0, x], self.three_a.at[d - 1], p.at(dx=d)
            )
        for d in range(1, NZ):
            z = (p.z + d) % NZ
            for part, first, i in (("b", 1, 0), ("c", 3, 1)):
                self.copies.start(
                    self.key(part + "3", d),
                    self.sums.at[first + z // 4, z % 4],
                    self.three_bc.at[i, d - 1],
                    p.at(dz=d),
                )

    def sum_third(self, out_ref):
        p = self.at
        rows = [self.sums[0, p.x].astype(F32)]
        for d in range(1, NX):
            self.copies.arrived(self.key("a3", d), self.three_a.at[d - 1], p.at(dx=-d))
            rows[0] += self.three_a[d - 1].astype(F32)
        for part, first, i in (("b", 1, 0), ("c", 3, 1)):
            value = self.sums[first + p.z // 4, p.z % 4].astype(F32)
            for d in range(1, NZ):
                self.copies.arrived(
                    self.key(part + "3", d), self.three_bc.at[i, d - 1], p.at(dz=-d)
                )
                value += self.three_bc[i, d - 1].astype(F32)
            rows.append(value)
        out_ref[...] = jnp.concatenate(rows, axis=0).T.astype(BF)


def scatter_kernel(
    hid_ref,
    grads_ref,
    gate_hbm,
    up_hbm,
    wd_ref,
    out_ref,
    in_ref,
    wgu,
    pairs,
    ring,
    stage,
    two,
    three_a,
    three_bc,
    sums,
    wsem,
    send,
    recv,
):
    p = Place()
    copies = Copies(send, recv)
    entered = enter(p.others())
    load_blocks(gate_hbm, lambda w: wgu.at[0, w], wsem.at[0])
    load_blocks(up_hbm, lambda w: wgu.at[1, w], wsem.at[0])

    def bufs(i):
        return (two.at[i], three_a.at[i], three_bc.at[i], sums.at[i])

    def lhs_in(w):
        return jnp.concatenate(
            [wgu[0, w].reshape(256, 256), wgu[1, w].reshape(256, 256)], axis=1
        )

    out = Scatter(
        "out", p, copies, lambda w: wd_ref[w].reshape(256, 256), lambda y, c: hid_ref[y, c],
        pairs.at[0], ring.at[0], stage, bufs(0),
    )
    inp = Scatter(
        "in", p, copies, lhs_in, lambda y, c: grads_ref[y, c],
        pairs.at[1], ring.at[1], stage, bufs(1),
    )
    entered()

    steps = [(out, j) for j in range(8)] + [(inp, j) for j in range(8)]
    sent = []

    def hand_over(n):
        which, j = steps[n]
        if n >= 2:
            for copy in sent[n - 2]:
                copy.wait_send()
        before = len(copies.sent)
        which.hand_over(j, n % 2)
        sent.append(copies.sent[before:])
        del copies.sent[before:]

    hand_over(0)
    hand_over(1)
    for m in range(7):
        out.send_round(m)
        if m < 6:
            hand_over(m + 2)
    pltpu.make_async_copy(wgu, wgu, wsem.at[0]).wait()
    hand_over(8)
    hand_over(9)
    inp.send_round(0)
    hand_over(10)
    out.finish_ring()
    out.send_second()
    for m in range(1, 7):
        inp.send_round(m)
        if m < 6:
            hand_over(m + 10)
        if m == 2:
            out.sum_second()
        if m == 4:
            out.sum_third(out_ref)
    inp.finish_ring()
    inp.send_second()
    inp.sum_second()
    inp.sum_third(in_ref)
    for group in sent[14:]:
        for copy in group:
            copy.wait_send()
    copies.drain()


def per_device(
    tokens, router_logits, routes, loss_weights, cotangent, gate_weight, up_weight, down_weight
):
    share = jax.nn.sigmoid(router_logits[:, 0] - router_logits[:, 1])
    experts = jnp.arange(8, dtype=jnp.int32)[:, None]
    combine = jnp.where(routes[None, :, 0] == experts, share[None, :], 0.0) + jnp.where(
        routes[None, :, 1] == experts, 1.0 - share[None, :], 0.0
    )
    scale = combine * (loss_weights.astype(F32) / 4096.0)[None, :]
    row = jnp.arange(8)[None, :, None]
    meta = jnp.where(row == 0, combine[:, None, :], jnp.where(row == 1, scale[:, None, :], 0.0))

    gate5 = gate_weight.reshape(NZ, NX, 3, FEAT, 256)
    up5 = up_weight.reshape(NZ, NX, 3, FEAT, 256)
    down2 = down_weight.reshape(256, 6144)
    vmem = pl.BlockSpec(memory_space=pltpu.VMEM)
    hbm = pl.BlockSpec(memory_space=pl.ANY)
    n_gather, n_scatter = 232, 288

    hid, grads, wd, dgrad = pl.pallas_call(
        gather_kernel,
        name="gather_hidden",
        out_shape=(
            jax.ShapeDtypeStruct((NY, 2, 256, TOK), BF),
            jax.ShapeDtypeStruct((NY, 2, 512, TOK), BF),
            jax.ShapeDtypeStruct((24, 4, 64, 256), BF),
            jax.ShapeDtypeStruct((256, 6144), BF),
        ),
        in_specs=[vmem, vmem, vmem, hbm, hbm, hbm],
        out_specs=(vmem, vmem, vmem, hbm),
        scratch_shapes=[
            pltpu.VMEM((2, 96, 256, TOK), BF),
            pltpu.VMEM((2, 96, 256, TOK), BF),
            pltpu.VMEM((24, 2, 4, 64, 256), BF),
            pltpu.VMEM((24, 256, 256), BF),
            pltpu.VMEM((256, 6144), BF),
            pltpu.VMEM((NY, 512, 256), F32),
            pltpu.VMEM((NY, 256, 256), F32),
            pltpu.VMEM((NY, 256, 256), BF),
            pltpu.VMEM((8, 8, TOK), F32),
            pltpu.SemaphoreType.DMA((2,)),
            pltpu.SemaphoreType.DMA,
            pltpu.SemaphoreType.DMA((n_gather,)),
            pltpu.SemaphoreType.DMA((n_gather,)),
        ],
        compiler_params=pltpu.CompilerParams(
            collective_id=1, has_side_effects=True, vmem_limit_bytes=60 * 2**20
        ),
    )(meta, tokens, cotangent, gate5, up5, down2)

    output, input_grad = pl.pallas_call(
        scatter_kernel,
        name="scatter_sums",
        out_shape=(
            jax.ShapeDtypeStruct((TOK, 192), BF),
            jax.ShapeDtypeStruct((TOK, 192), BF),
        ),
        in_specs=[vmem, vmem, hbm, hbm, vmem],
        out_specs=(vmem, vmem),
        scratch_shapes=[
            pltpu.VMEM((2, 24, 4, 64, 256), BF),
            pltpu.VMEM((2, 96, 256, TOK), BF),
            pltpu.VMEM((2, 6, 7, 2, 256, TOK), BF),
            pltpu.VMEM((2, 12, 256, TOK), BF),
            pltpu.VMEM((2, 3, 5, 256, TOK), BF),
            pltpu.VMEM((2, 3, 64, TOK), BF),
            pltpu.VMEM((2, 2, 7, 64, TOK), BF),
            pltpu.VMEM((2, 5, 4, 64, TOK), BF),
            pltpu.SemaphoreType.DMA((1,)),
            pltpu.SemaphoreType.DMA((n_scatter,)),
            pltpu.SemaphoreType.DMA((n_scatter,)),
        ],
        compiler_params=pltpu.CompilerParams(
            collective_id=2, has_side_effects=True, vmem_limit_bytes=60 * 2**20
        ),
    )(hid, grads, gate5, up5, wd)
    return (output, input_grad, dgrad.reshape(1, 256, 6144))


def solution(mesh):
    in_specs = (
        P("segment", "fsdp"),
        P("segment", None),
        P("segment", None),
        P("segment"),
        P("segment", "fsdp"),
        P("segment", None, "fsdp"),
        P("segment", None, "fsdp"),
        P("segment", "fsdp", None),
    )
    out_specs = (P("segment", "fsdp"), P("segment", "fsdp"), P("segment", "fsdp", None))
    return jax.shard_map(
        per_device, mesh=mesh, in_specs=in_specs, out_specs=out_specs, check_vma=False
    )
```

time: 746 us -> 227 us (0.30)
  waiting for transfers between devices: 537 us -> 0 us
  Pallas kernels: 0 us -> 216 us
  local copies, waits for them, and re-layouts: 109 us -> 8.61 us
  matrix products: 45.5 us -> 0 us
  blocking collectives: 21.9 us -> 0 us
  between operations: 14 us -> 0.66 us
  starting transfers between devices: 10 us -> 0 us
    unnamed x6 -> x0, waiting for transfers between devices: 370 us -> none
    pallas_call x0 -> x2, Pallas kernels: none -> 216 us  [the longest x1 121 us: per_device(): pl.pallas_call(scatter_kernel, name='scatter_sums', out_shape=(jax.ShapeD...]
    all_gather x2 -> x0, waiting for transfers between devices: 162 us -> none  [the longest x1 102 us: per_device(): lax.all_gather(came_rows, 'fsdp', axis=2, tiled=True)]
    unnamed x26 -> x7, local copies, waits for them, and re-layouts: 71.2 us -> 7.86 us
    dot_general x11 -> x0, matrix products: 45.5 us -> none  [the longest x1 9.1 us: expert_backward(): lax.dot_general(up_grad, up_part, contract_last, preferred_element_type=j...]
    all_gather x2 -> x0, local copies, waits for them, and re-layouts: 28.1 us -> none  [the longest x1 14.1 us: per_device(): lax.all_gather(came_rows, 'fsdp', axis=2, tiled=True)]
    all_to_all x2 -> x0, blocking collectives: 21.9 us -> none  [the longest x1 11.3 us: per_device(): lax.all_to_all(send_rows, 'segment', split_axis=0, concat_axis=0, tiled=T...]
    all_to_all x2 -> x0, starting transfers between devices: 9.68 us -> none  [the longest x1 4.85 us: per_device(): lax.all_to_all(out_sum.astype(jnp.bfloat16), 'segment', split_axis=0, con...]
  transfers between devices with their start and end apart: 6 -> 0, of which waited for: 5 -> 0; matrix products, arithmetic and copies ran while one was open for 20% -> 0% of each run, Pallas kernels for 0% -> 0%
where the time goes in v1:
time: 227 us
  Pallas kernels  216 us (95%)
  local copies, waits for them, and re-layouts  8.61 us (4%)
    pallas_call x1, Pallas kernels, per_device(): pl.pallas_call(scatter_kernel, name='scatter_sums', out_shape=(jax.ShapeD...  121 us
    pallas_call x1, Pallas kernels, per_device(): pl.pallas_call(gather_kernel, name='gather_hidden', out_shape=(jax.ShapeD...  95 us
    unnamed x7, local copies, waits for them, and re-layouts  7.86 us

profile of v1, /device:TPU:8, one launch (start us, length us, event | category | flops | bytes accessed | tf_op | source)
XLA Modules:
  0.0 226.8 jit_solution(7180309671701980279)
XLA Ops:
  0.6 0.8 slice_bitcast_fusion.1
  1.4 0.8 broadcast_subtract_fusion
  2.2 0.7 select_select_fusion.meta_ref
  2.9 1.5 copy.11.tok_ref
  4.4 1.5 copy.12.cot_ref
  5.9 95.0 %gather_hidden.1 = (bf16[4,2,256,128]{3,2,1,0:T(8,128)(2,1)}, bf16[4,2,512,128]{3,2,1,0:T(8,128)(2,1)}, bf16[24,4,64,256]{3,2,1,0:T(8,128)(2,1)}, bf16[256,6144]{1,0:T(8,128)(2,1)}) custom-call(f32[8,8,128]{2,1,0:T(8,128)} %select_select_fusion.meta_ref, bf16[128,192]{1,0:T(8,128)(2,1)} %copy.11.tok_ref, bf16[128,192]{1,0:T(8,128)(2,1)} %copy.12.cot_ref, ...), custom_call_target="tpu_custom_call" | custom-call | tf_op jit(solution)/shard_map/gather_hidden/pallas_call | solution.py:807
  100.9 0.0 copy-start
  100.9 121.1 %scatter_sums.1 = (bf16[128,192]{1,0:T(8,128)(2,1)}, bf16[128,192]{1,0:T(8,128)(2,1)}) custom-call(bf16[4,2,256,128]{3,2,1,0:T(8,128)(2,1)} %get-tuple-element.9.hid_ref, bf16[4,2,512,128]{3,2,1,0:T(8,128)(2,1)} %get-tuple-element.10.grads_ref, bf16[8,4,3,64,256]{4,3,2,1,0:T(8,128)(2,1)} %bitcast.12, bf16[8,4,3,64,256]{4,3,2,1,0:T(8,128)(2,1)} %bitcast.14, ...), custom_call_target="tpu_custom_call" | custom-call | tf_op jit(solution)/shard_map/scatter_sums/pallas_call | solution.py:838
  222.0 1.6 copy.13
  223.5 1.6 copy.14
  225.1 0.0 copy-done
  225.1 1.7 copy.16
  (2 shorter events, 0.0 us)
Async XLA Ops:
  100.9 124.2 %copy-start = (bf16[256,6144]{1,0:T(8,128)(2,1)S(1)}, bf16[256,6144]{1,0:T(8,128)(2,1)}, u32[]{:S(2)}) copy-start(bf16[256,6144]{1,0:T(8,128)(2,1)} %get-tuple-element.14) | copy-start | bytes 9437188

commit v2 on v1

--- a/solution.py
+++ b/solution.py
@@ -11,6 +11,7 @@
 BF = jnp.bfloat16
 F32 = jnp.float32
 NX, NY, NZ = 4, 4, 8
+SLOTS = 6
 FEAT, TOK = 64, 128
 
 
@@ -51,15 +52,26 @@
     return lambda: pl.semaphore_wait(barrier, len(devices))
 
 
-def a_base(y, z, half):
-    return z * 4 + 2 * half
-
-
-def brick_of(bases, t):
-    base = bases[0]
-    for k in range(1, len(bases)):
-        base = jnp.where(t // 2 == k, bases[k], base)
-    return base + t % 2
+SIZE = {"a": 1, "b": 2, "c": 2}
+PARTS = ("a", "b", "c")
+
+
+def ring_to(p, part, sign):
+    return {"a": p.at(dz=sign), "b": p.at(dx=sign), "c": p.at(dy=sign)}[part]
+
+
+def gather_order(part, sign):
+    hops = 3 if part == "a" else 1
+    rows, last = ((0, 1, 3, 2), (0, 1)) if sign > 0 else ((0, 3, 2, 1), (3, 2))
+    return [(h, r) for h in range(1, hops + 1) for r in rows] + [(hops + 1, r) for r in last]
+
+
+def scatter_order(part, sign):
+    if part == "a":
+        rows, last = ((0, 1, 2, 3), (2, 3)) if sign > 0 else ((2, 3, 0, 1), (0, 1))
+        return [(4, r) for r in last] + [(h, r) for h in (3, 2, 1) for r in rows]
+    rows, last = ((1, 2, 3, 0), (2, 0)) if sign > 0 else ((2, 1, 3, 0), (1, 3))
+    return [(2, r) for r in last] + [(1, r) for r in rows]
 
 
 def weight_of(b):
@@ -174,117 +186,102 @@
             block, device = self.second(part, d)
             self.copies.arrived(self.key(part + "2", d), block, device)
 
-    def chunk(self, base):
-        return self.buf.at[self.at.c, pl.ds(base, 2)]
-
-    def neighbour(self, part, sign):
-        p = self.at
-        return {"a": p.at(dz=sign), "b": p.at(dx=sign), "c": p.at(dy=sign)}[part]
-
-    def base(self, part, sign, m):
+    def chunk(self, part, base):
+        return self.buf.at[self.at.c, pl.ds(base, SIZE[part])]
+
+    def base(self, part, back, rel):
         p = self.at
         if part == "a":
-            z = (p.z - sign * (1 + m // 2)) % NZ
-            half = m % 2 if sign > 0 else 1 - m % 2
-            return z * 4 + 2 * half
-        hop = 1 if m < 4 else 2
-        q = m % 4 if sign > 0 else (m + 2) % 4
+            return ((p.z - back) % NZ) * 4 + (p.y + rel) % NY
         if part == "b":
-            return 32 + (((p.x - sign * hop) % NX) * 4 + q) * 2
-        return 64 + (((p.y - sign * hop) % NY) * 4 + q) * 2
-
-    def own_base(self, part, sign, m):
-        p = self.at
-        if part == "a":
-            return p.z * 4 + 2 * (m % 2 if sign > 0 else 1 - m % 2)
-        q = m % 4 if sign > 0 else (m + 2) % 4
-        if part == "b":
-            return 32 + (p.x * 4 + q) * 2
-        return 64 + (p.y * 4 + q) * 2
-
-    def own_span(self, part):
-        p = self.at
-        if part == "a":
-            return self.buf.at[p.c, pl.ds(p.z * 4, 4)]
-        if part == "b":
-            return self.buf.at[p.c, pl.ds(32 + p.x * 8, 8)]
-        return self.buf.at[p.c, pl.ds(64 + p.y * 8, 8)]
-
-    def other_span(self, part):
-        p = self.at
-        if part == "a":
-            return self.buf.at[1 - p.c, pl.ds(p.z * 4, 4)]
-        if part == "b":
-            return self.buf.at[1 - p.c, pl.ds(32 + p.x * 8, 8)]
-        return self.buf.at[1 - p.c, pl.ds(64 + p.y * 8, 8)]
-
-    def start_ring(self, part):
-        for m in range(2 if part == "a" else 4):
+            return 32 + (((p.x - back) % NX) * 4 + (p.y + rel) % NY) * 2
+        return 64 + (((p.y - back) % NY) * 4 + (p.x + rel) % NX) * 2
+
+    def span(self, part, c):
+        p = self.at
+        first, count = {
+            "a": (p.z * 4, 4), "b": (32 + p.x * 8, 8), "c": (64 + p.y * 8, 8)
+        }[part]
+        return self.buf.at[c, pl.ds(first, count)]
+
+    def send_own(self, part, rels):
+        for rel in rels:
+            ref = self.chunk(part, self.base(part, 0, rel))
             for sign in (1, -1):
-                ref = self.chunk(self.own_base(part, sign, m))
-                self.copies.start(self.key(part, sign, m), ref, ref, self.neighbour(part, sign))
-        ref = self.own_span(part)
+                self.copies.start(self.key(part, sign, 1, rel), ref, ref, ring_to(self.at, part, sign))
+
+    def finish_second(self, part):
+        for rel in (1, 3, 2):
+            d = (4 - rel) % 4
+            block, device = self.second(part, d)
+            self.copies.arrived(self.key(part + "2", d), block, device)
+            self.send_own(part, (rel,))
+        ref = self.span(part, self.at.c)
         self.copies.start(self.key("own", part), ref, ref, self.at.at(sibling=True))
 
-    def messages(self, m):
-        return [
-            (part, sign)
-            for part in ("a", "b", "c")
-            if m < (7 if part == "a" else 6)
-            for sign in (1, -1)
-        ]
-
-    def bases(self, m):
-        return [self.base(part, sign, m) for part, sign in self.messages(m)]
-
-    def ring_round(self, m):
-        for part, sign in self.messages(m):
-            ref = self.chunk(self.base(part, sign, m))
-            self.copies.arrived(self.key(part, sign, m), ref, self.neighbour(part, -sign))
-            step = 2 if part == "a" else 4
-            if m + step < (7 if part == "a" else 6):
+    def messages(self, s):
+        found = [("a", sign) + gather_order("a", sign)[s] for sign in (1, -1)]
+        part, n = ("b", "c")[s % 2], s // 2
+        if n < 6:
+            found += [(part, sign) + gather_order(part, sign)[n] for sign in (1, -1)]
+        return found
+
+    def ring_round(self, s):
+        for part, sign, hop, rel in self.messages(s):
+            ref = self.chunk(part, self.base(part, sign * hop, rel))
+            self.copies.arrived(self.key(part, sign, hop, rel), ref, ring_to(self.at, part, -sign))
+            if (hop + 1, rel) in gather_order(part, sign):
                 self.copies.start(
-                    self.key(part, sign, m + step), ref, ref, self.neighbour(part, sign)
+                    self.key(part, sign, hop + 1, rel), ref, ref, ring_to(self.at, part, sign)
                 )
-            self.copies.start(self.key("sib", part, sign, m), ref, ref, self.at.at(sibling=True))
-
-    def wait_other(self, m):
-        p = self.at
-        for part, sign in self.messages(m):
-            ref = self.buf.at[1 - p.c, pl.ds(self.base(part, sign, m), 2)]
-            self.copies.arrived(self.key("sib", part, sign, m), ref, p.at(sibling=True))
+            self.copies.start(
+                self.key("sib", part, sign, hop, rel), ref, ref, self.at.at(sibling=True)
+            )
+
+    def wait_other(self, s):
+        p = self.at
+        for part, sign, hop, rel in self.messages(s):
+            ref = self.buf.at[1 - p.c, pl.ds(self.base(part, sign * hop, rel), SIZE[part])]
+            self.copies.arrived(self.key("sib", part, sign, hop, rel), ref, p.at(sibling=True))
 
     def wait_other_own(self):
         for part in ("a", "b", "c"):
             self.copies.arrived(
-                self.key("own", part), self.other_span(part), self.at.at(sibling=True)
+                self.key("own", part), self.span(part, 1 - self.at.c), self.at.at(sibling=True)
             )
 
-    def multiply(self, weights, total, bricks, count):
+    def both(self, b):
+        return jnp.concatenate([self.buf[0, b], self.buf[1, b]], axis=1)
+
+    def multiply_single(self, weights, total, b):
+        total[b % 4] += dot(weights(b // 4), self.both(b))
+
+    def multiply_chunk(self, weights, total, b):
+        w = weight_of(b)
+        rhs = jnp.concatenate([self.both(b), self.both(b + 1)], axis=0)
+        total[row_of(b)] += dot(jnp.concatenate([weights(w), weights(w + 1)], axis=1), rhs)
+
+    def multiply_own(self, weights, total):
+        p = self.at
+
         def step(t, carry):
-            b = bricks(t)
-            row = row_of(b)
-            rhs = jnp.concatenate([self.buf[0, b], self.buf[1, b]], axis=1)
-            total[row] += dot(weights(weight_of(b)), rhs)
+            self.multiply_single(weights, total, p.z * 4 + t)
+            self.multiply_chunk(weights, total, 32 + p.x * 8 + 2 * t)
+            self.multiply_chunk(weights, total, 64 + p.y * 8 + 2 * t)
             return carry
 
-        lax.fori_loop(0, count, step, 0)
-
-    def multiply_own(self, weights, total):
-        p = self.at
-
-        def bricks(t):
-            return jnp.where(
-                t < 4,
-                p.z * 4 + t,
-                jnp.where(t < 12, 32 + p.x * 8 + t - 4, 64 + p.y * 8 + t - 12),
-            )
-
-        self.multiply(weights, total, bricks, 20)
-
-    def multiply_round(self, weights, total, m):
-        bases = self.bases(m)
-        self.multiply(weights, total, lambda t: brick_of(bases, t), 2 * len(bases))
+        lax.fori_loop(0, 4, step, 0)
+
+    def multiply_round(self, weights, total, s):
+        bases = [self.base(part, sign * hop, rel) for part, sign, hop, rel in self.messages(s)]
+
+        def step(t, carry):
+            self.multiply_single(weights, total, jnp.where(t == 0, bases[0], bases[1]))
+            if len(bases) > 2:
+                self.multiply_chunk(weights, total, jnp.where(t == 0, bases[2], bases[3]))
+            return carry
+
+        lax.fori_loop(0, 2, step, 0)
 
 
 def load_blocks(hbm, part_ref, sem):
@@ -335,8 +332,8 @@
     load_blocks(up_hbm, lambda w: wgu.at[w, 1], wsem.at[0])
     pltpu.make_async_copy(down_hbm, flat, wsem.at[1]).start()
 
-    tok.put_own(tok_ref[...].astype(F32).T.astype(BF))
-    cot.put_own(cot_ref[...].astype(F32).T.astype(BF))
+    tok.put_own(tok_ref)
+    cot.put_own(cot_ref)
     meta[p.seg] = meta_ref[p.seg]
     total[...] = jnp.zeros_like(total)
     hgrad[...] = jnp.zeros_like(hgrad)
@@ -345,31 +342,12 @@
     tok.send_first()
     for d in range(1, 8):
         copies.start(("meta", d), meta_ref.at[(p.seg + d) % 8], meta.at[p.seg], far[d - 1])
-
-    pltpu.make_async_copy(wgu, wgu, wsem.at[0]).wait()
 
     def turn_gu(w, carry):
         for k in range(2):
             block = wgu[w, k].reshape(256, 256)
             wgu[w, k] = block.T.reshape(4, 64, 256)
         return carry
-
-    lax.fori_loop(0, 6, turn_gu, 0)
-    tok.wait_first_a()
-    tok.send_second("a")
-    lax.fori_loop(6, 12, turn_gu, 0)
-    tok.wait_first_bc()
-    tok.send_second("b")
-    tok.send_second("c")
-    tok.wait_second("a")
-    tok.start_ring("a")
-    cot.send_first()
-    lax.fori_loop(12, 24, turn_gu, 0)
-    tok.wait_second("b")
-    tok.start_ring("b")
-    tok.wait_second("c")
-    tok.start_ring("c")
-    pltpu.make_async_copy(down_hbm, flat, wsem.at[1]).wait()
 
     def turn_down(i, carry):
         block = flat[:, pl.ds(mult(i * 384, 384), 384)].T
@@ -391,33 +369,54 @@
     def w_down(w):
         return wdt[w]
 
-    for m in range(7):
-        tok.ring_round(m)
-        if m == 0:
+    tok.wait_first_a()
+    tok.send_own("a", (0,))
+    tok.send_second("a")
+    pltpu.make_async_copy(wgu, wgu, wsem.at[0]).wait()
+    lax.fori_loop(0, 4, turn_gu, 0)
+    tok.finish_second("a")
+    tok.wait_first_bc()
+    tok.send_own("b", (0,))
+    tok.send_own("c", (0,))
+    tok.send_second("b")
+    tok.send_second("c")
+    cot.send_first()
+    lax.fori_loop(4, 8, turn_gu, 0)
+    lax.fori_loop(8, 14, turn_gu, 0)
+    tok.finish_second("b")
+    tok.finish_second("c")
+    lax.fori_loop(14, 24, turn_gu, 0)
+    pltpu.make_async_copy(down_hbm, flat, wsem.at[1]).wait()
+
+    for s in range(14):
+        tok.ring_round(s)
+        if s == 0:
             tok.wait_other_own()
             tok.multiply_own(w_gu, total)
         else:
-            tok.wait_other(m - 1)
-            tok.multiply_round(w_gu, total, m - 1)
-        if m == 1:
+            tok.wait_other(s - 1)
+            tok.multiply_round(w_gu, total, s - 1)
+        if s == 2:
             cot.wait_first_a()
             cot.send_second("a")
             cot.wait_first_bc()
             cot.send_second("b")
             cot.send_second("c")
-            lax.fori_loop(0, 8, turn_down, 0)
-        if m == 2:
-            lax.fori_loop(8, 16, turn_down, 0)
-        if m == 3:
-            lax.fori_loop(0, 12, turn_back, 0)
-        if m == 4:
-            for part in ("a", "b", "c"):
-                cot.wait_second(part)
-                cot.start_ring(part)
-            lax.fori_loop(12, 24, turn_back, 0)
+        if 3 <= s < 7:
+            lax.fori_loop(4 * s - 12, 4 * s - 8, turn_down, 0)
+        if 7 <= s < 10:
+            lax.fori_loop(8 * s - 56, 8 * s - 48, turn_back, 0)
+        if s == 6:
+            cot.send_own("b", (0,))
+            cot.finish_second("b")
+            cot.send_own("c", (0,))
+            cot.finish_second("c")
+        if s == 9:
+            cot.send_own("a", (0,))
+            cot.finish_second("a")
     cot.ring_round(0)
-    tok.wait_other(6)
-    tok.multiply_round(w_gu, total, 6)
+    tok.wait_other(13)
+    tok.multiply_round(w_gu, total, 13)
     for d in range(1, 8):
         copies.arrived(("meta", d), meta.at[(p.seg - d) % 8], far[7 - d])
 
@@ -442,17 +441,17 @@
 
     lax.fori_loop(0, 16, activate, 0)
 
-    for m in range(7):
-        if m > 0:
-            cot.ring_round(m)
-        if m == 0:
+    for s in range(14):
+        if s > 0:
+            cot.ring_round(s)
+        if s == 0:
             cot.wait_other_own()
             cot.multiply_own(w_down, hgrad)
         else:
-            cot.wait_other(m - 1)
-            cot.multiply_round(w_down, hgrad, m - 1)
-    cot.wait_other(6)
-    cot.multiply_round(w_down, hgrad, 6)
+            cot.wait_other(s - 1)
+            cot.multiply_round(w_down, hgrad, s - 1)
+    cot.wait_other(13)
+    cot.multiply_round(w_down, hgrad, 13)
 
     def backward(i, carry):
         y, r = i // 4, i % 4
@@ -493,141 +492,132 @@
     out.wait()
 
 
-RING = (("a", 1), ("a", -1), ("b", 1), ("b", -1), ("c", 1), ("c", -1))
-
-
 class Scatter:
-    def __init__(self, name, place, copies, lhs, rhs, pairs, ring, stage, bufs):
-        self.name, self.at, self.copies = name, place, copies
-        self.lhs, self.rhs, self.pairs, self.ring, self.stage = lhs, rhs, pairs, ring, stage
+    def __init__(
+        self, name, first, place, copies, lhs, rhs, pairs, ring_a, ring_bc, mine, stage, bufs
+    ):
+        self.name, self.first, self.at, self.copies = name, first, place, copies
+        self.lhs, self.rhs, self.pairs = lhs, rhs, pairs
+        self.ring_a, self.ring_bc, self.mine, self.stage = ring_a, ring_bc, mine, stage
         self.two, self.three_a, self.three_bc, self.sums = bufs
 
     def key(self, *rest):
         return (self.name,) + rest
 
-    def base(self, part, sign, m):
+    def base(self, part, ahead, rel):
         p = self.at
         if part == "a":
-            hop = 4 - (m + 1) // 2
-            half = m % 2 if sign > 0 else 1 - m % 2
-            return ((p.z + sign * hop) % NZ) * 4 + 2 * half
-        hop = 2 if m < 2 else 1
-        q = m % 4 if sign > 0 else (m + 2) % 4
+            return ((p.z + ahead) % NZ) * 4 + (p.y + rel) % NY
         if part == "b":
-            return 32 + (((p.x + sign * hop) % NX) * 4 + q) * 2
-        return 64 + (((p.y + sign * hop) % NY) * 4 + q) * 2
-
-    def own(self, part, q):
-        p = self.at
-        if part == "a":
-            return p.z * 4 + 2 * q
-        if part == "b":
-            return 32 + (p.x * 4 + q) * 2
-        return 64 + (p.y * 4 + q) * 2
-
-    def groups(self, j):
-        if j < 6:
-            return [self.base(part, sign, j) for part, sign in RING]
-        if j == 6:
-            return [self.base("a", 1, 6), self.base("a", -1, 6)] + [
-                self.own(part, q) for part in ("a", "b") for q in range(2)
-            ]
-        return [self.own("b", 2), self.own("b", 3)] + [self.own("c", q) for q in range(4)]
-
-    def keys(self, j):
-        if j < 6:
-            return [(part, sign, j) for part, sign in RING]
-        if j == 6:
-            return [("a", 1, 6), ("a", -1, 6)] + [
-                ("own", part, q) for part in ("a", "b") for q in range(2)
-            ]
-        return [("own", "b", 2), ("own", "b", 3)] + [("own", "c", q) for q in range(4)]
-
-    def product(self, b, c):
-        return dot(self.lhs(weight_of(b)), self.rhs(row_of(b), c))
-
-    def hand_over(self, j, slot):
-        p = self.at
-        bases = self.groups(j)
+            return 32 + (((p.x + ahead) % NX) * 4 + (p.y + rel) % NY) * 2
+        return 64 + (((p.y + ahead) % NY) * 4 + (p.x + rel) % NX) * 2
+
+    def chunks(self, j):
+        found = []
+        for i, sign in enumerate((1, -1)):
+            if j < 14:
+                found.append(("a", sign) + scatter_order("a", sign)[j])
+            else:
+                found.append(("a", 0, 0, ((1, 2), (3, 0))[j - 14][i]))
+        part, n = ("b", "c")[j % 2], j // 2
+        for i, sign in enumerate((1, -1)):
+            if n < 6:
+                found.append((part, sign) + scatter_order(part, sign)[n])
+            else:
+                found.append((part, 0, 0, ((1, 2), (3, 0))[n - 6][i]))
+        return found
+
+    def place_of(self, chunk):
+        for j in range(16):
+            chunks = self.chunks(j)
+            if chunk in chunks:
+                k = chunks.index(chunk)
+                return (self.first + j) % SLOTS, (0, 1, 2, 4)[k]
+
+    def produce(self, j):
+        p = self.at
+        slot = (self.first + j) % SLOTS
+        chunks = self.chunks(j)
+        bases = [self.base(part, sign * hop, rel) for part, sign, hop, rel in chunks]
+
+        def one(w, rhs, at):
+            value = dot(self.lhs(w), rhs).astype(BF)
+            self.mine[slot, at] = value[:, 0:TOK]
+            self.stage[slot, at] = value[:, TOK:]
+
+        def rhs_of(row):
+            return jnp.concatenate([self.rhs(row, p.c), self.rhs(row, 1 - p.c)], axis=1)
 
         def step(t, carry):
-            b = brick_of(bases, t)
-            self.stage[slot, t] = self.product(b, 1 - p.c).astype(BF)
+            b = jnp.where(t == 0, bases[0], bases[1])
+            one(b // 4, rhs_of(b % 4), t)
+            b = jnp.where(t == 0, bases[2], bases[3])
+            w, rhs = weight_of(b), rhs_of(row_of(b))
+            one(w, rhs, 2 + 2 * t)
+            one(w + 1, rhs, 3 + 2 * t)
             return carry
 
-        lax.fori_loop(0, 12, step, 0)
-        for k, (key, base) in enumerate(zip(self.keys(j), bases)):
+        lax.fori_loop(0, 2, step, 0)
+        for chunk, base in zip(chunks, bases):
+            _, at = self.place_of(chunk)
+            size = SIZE[chunk[0]]
             self.copies.start(
-                self.key("sib") + key,
-                self.stage.at[slot, pl.ds(2 * k, 2)],
-                self.pairs.at[pl.ds(base, 2)],
+                self.key("sib") + chunk,
+                self.stage.at[slot, pl.ds(at, size)],
+                self.pairs.at[pl.ds(base, size)],
                 p.at(sibling=True),
             )
 
-    def handed(self, key, base):
-        self.copies.arrived(
-            self.key("sib") + key, self.pairs.at[pl.ds(base, 2)], self.at.at(sibling=True)
-        )
-
-    def neighbour(self, part, sign):
-        p = self.at
-        return {"a": p.at(dz=sign), "b": p.at(dx=sign), "c": p.at(dy=sign)}[part]
-
-    def came(self, k, m):
-        part, sign = RING[k]
-        self.copies.arrived(
-            self.key(part, sign, m), self.ring.at[k, m], self.neighbour(part, -sign)
-        )
-
-    def send_round(self, m):
-        p = self.at
-        for k, (part, sign) in enumerate(RING):
-            if m >= (7 if part == "a" else 6):
+    def landing(self, part, sign, i):
+        side = 0 if sign > 0 else 1
+        if part == "a":
+            return self.ring_a.at[side, pl.ds(i, 1)]
+        return self.ring_bc.at[("b", "c").index(part), side, pl.ds(2 * i, 2)]
+
+    def came(self, part, sign, i):
+        ref = self.landing(part, sign, i)
+        self.copies.arrived(self.key(part, sign, i), ref, ring_to(self.at, part, -sign))
+        return ref
+
+    def gather_up(self, chunk, base, arrivals):
+        part = chunk[0]
+        size = SIZE[part]
+        ref = self.pairs.at[pl.ds(base, size)]
+        self.copies.arrived(self.key("sib") + chunk, ref, self.at.at(sibling=True))
+        slot, at = self.place_of(chunk)
+        refs = [self.came(part, sign, i) for sign, i in arrivals]
+        for t in range(size):
+            value = self.mine[slot, at + t].astype(F32) + self.pairs[base + t].astype(F32)
+            for came in refs:
+                value += came[t].astype(F32)
+            self.pairs[base + t] = value.astype(BF)
+        return ref
+
+    def send_round(self, s):
+        for chunk in self.chunks(s):
+            part, sign, hop, rel = chunk
+            if sign == 0:
                 continue
-            base = self.base(part, sign, m)
-            self.handed((part, sign, m), base)
-            back = m - (2 if part == "a" else 4)
-            if back >= 0:
-                self.came(k, back)
-
-            def step(t, carry):
-                b = base + t
-                value = self.product(b, p.c) + self.pairs[b].astype(F32)
-                if back >= 0:
-                    value += self.ring[k, back, t].astype(F32)
-                self.pairs[b] = value.astype(BF)
-                return carry
-
-            lax.fori_loop(0, 2, step, 0)
+            order = scatter_order(part, sign)
+            arrivals = [(sign, order.index((hop + 1, rel)))] if (hop + 1, rel) in order else []
+            i = order.index((hop, rel))
+            ref = self.gather_up(chunk, self.base(part, sign * hop, rel), arrivals)
             self.copies.start(
-                self.key(part, sign, m),
-                self.pairs.at[pl.ds(base, 2)],
-                self.ring.at[k, m],
-                self.neighbour(part, sign),
+                self.key(part, sign, i), ref, self.landing(part, sign, i), ring_to(self.at, part, sign)
             )
 
-    def finish_ring(self):
-        p = self.at
-        for part, first, count in (("a", 0, 2), ("b", 2, 4), ("c", 4, 4)):
-            for q in range(count):
-                base = self.own(part, q)
-                self.handed(("own", part, q), base)
-                if part == "a":
-                    plus, minus = 6 - q, 5 + q
-                else:
-                    plus, minus = 2 + (q + 2) % 4, 2 + q
-                self.came(first, plus)
-                self.came(first + 1, minus)
-
-                def step(t, carry):
-                    b = base + t
-                    value = self.product(b, p.c) + self.pairs[b].astype(F32)
-                    value += self.ring[first, plus, t].astype(F32)
-                    value += self.ring[first + 1, minus, t].astype(F32)
-                    self.pairs[b] = value.astype(BF)
-                    return carry
-
-                lax.fori_loop(0, 2, step, 0)
+    def finish_ring(self, part, rels):
+        for rel in rels:
+            arrivals = [(sign, scatter_order(part, sign).index((1, rel))) for sign in (1, -1)]
+            self.gather_up((part, 0, 0, rel), self.base(part, 0, rel), arrivals)
+            if rel:
+                bricks, slot, device = self.second(part, rel)
+                self.copies.start(
+                    self.key(part + "2", rel),
+                    self.pairs.at[bricks],
+                    self.two.at[rel - 1, slot],
+                    device,
+                )
 
     def second(self, part, d):
         p = self.at
@@ -636,17 +626,6 @@
         if part == "b":
             return pl.ds(32 + (p.x * 4 + (p.y + d) % NY) * 2, 2), pl.ds(1, 2), p.at(dy=d)
         return pl.ds(64 + (p.y * 4 + (p.x + d) % NX) * 2, 2), pl.ds(3, 2), p.at(dx=d)
-
-    def send_second(self):
-        for part in ("a", "b", "c"):
-            for d in range(1, 4):
-                bricks, slot, device = self.second(part, d)
-                self.copies.start(
-                    self.key(part + "2", d),
-                    self.pairs.at[bricks],
-                    self.two.at[d - 1, slot],
-                    device,
-                )
 
     def sum_second(self):
         p = self.at
@@ -694,7 +673,8 @@
                 )
                 value += self.three_bc[i, d - 1].astype(F32)
             rows.append(value)
-        out_ref[...] = jnp.concatenate(rows, axis=0).T.astype(BF)
+        for k in range(3):
+            out_ref[k * FEAT : (k + 1) * FEAT] = rows[k].astype(BF)
 
 
 def scatter_kernel(
@@ -707,7 +687,9 @@
     in_ref,
     wgu,
     pairs,
-    ring,
+    ring_a,
+    ring_bc,
+    mine,
     stage,
     two,
     three_a,
@@ -732,54 +714,67 @@
         )
 
     out = Scatter(
-        "out", p, copies, lambda w: wd_ref[w].reshape(256, 256), lambda y, c: hid_ref[y, c],
-        pairs.at[0], ring.at[0], stage, bufs(0),
+        "out", 0, p, copies, lambda w: wd_ref[w].reshape(256, 256), lambda y, c: hid_ref[y, c],
+        pairs.at[0], ring_a.at[0], ring_bc.at[0], mine, stage, bufs(0),
     )
     inp = Scatter(
-        "in", p, copies, lhs_in, lambda y, c: grads_ref[y, c],
-        pairs.at[1], ring.at[1], stage, bufs(1),
+        "in", 16, p, copies, lhs_in, lambda y, c: grads_ref[y, c],
+        pairs.at[1], ring_a.at[1], ring_bc.at[1], mine, stage, bufs(1),
     )
     entered()
 
-    steps = [(out, j) for j in range(8)] + [(inp, j) for j in range(8)]
+    steps = [(out, j) for j in range(16)] + [(inp, j) for j in range(16)]
     sent = []
 
-    def hand_over(n):
+    def produce(n):
         which, j = steps[n]
-        if n >= 2:
-            for copy in sent[n - 2]:
+        if n >= SLOTS:
+            for copy in sent[n - SLOTS]:
                 copy.wait_send()
         before = len(copies.sent)
-        which.hand_over(j, n % 2)
+        which.produce(j)
         sent.append(copies.sent[before:])
         del copies.sent[before:]
 
-    hand_over(0)
-    hand_over(1)
-    for m in range(7):
-        out.send_round(m)
-        if m < 6:
-            hand_over(m + 2)
+    for n in range(2):
+        produce(n)
+    for s in range(14):
+        out.send_round(s)
+        produce(s + 2)
+        if s == 12:
+            out.finish_ring("b", (1, 2))
+        if s == 13:
+            out.finish_ring("c", (1, 2))
     pltpu.make_async_copy(wgu, wgu, wsem.at[0]).wait()
-    hand_over(8)
-    hand_over(9)
+    produce(16)
     inp.send_round(0)
-    hand_over(10)
-    out.finish_ring()
-    out.send_second()
-    for m in range(1, 7):
-        inp.send_round(m)
-        if m < 6:
-            hand_over(m + 10)
-        if m == 2:
+    produce(17)
+    inp.send_round(1)
+    out.finish_ring("a", (1, 2))
+    out.finish_ring("b", (3, 0))
+    produce(18)
+    inp.send_round(2)
+    out.finish_ring("a", (3, 0))
+    out.finish_ring("c", (3, 0))
+    produce(19)
+    for s in range(3, 14):
+        inp.send_round(s)
+        produce(s + 17)
+        if s == 4:
             out.sum_second()
-        if m == 4:
+        if s == 7:
             out.sum_third(out_ref)
-    inp.finish_ring()
-    inp.send_second()
+        if s == 12:
+            inp.finish_ring("b", (1, 2))
+        if s == 13:
+            inp.finish_ring("c", (1, 2))
+    produce(31)
+    inp.finish_ring("b", (3, 0))
+    inp.finish_ring("c", (3, 0))
+    inp.finish_ring("a", (1, 2, 3, 0))
     inp.sum_second()
     inp.sum_third(in_ref)
-    for group in sent[14:]:
+    for group in sent[32 - SLOTS :]:
         for copy in group:
             copy.wait_send()
     copies.drain()
@@ -802,7 +797,7 @@
     down2 = down_weight.reshape(256, 6144)
     vmem = pl.BlockSpec(memory_space=pltpu.VMEM)
     hbm = pl.BlockSpec(memory_space=pl.ANY)
-    n_gather, n_scatter = 232, 288
+    n_gather, n_scatter = 288, 288
 
     hid, grads, wd, dgrad = pl.pallas_call(
         gather_kernel,
@@ -833,22 +828,24 @@
         compiler_params=pltpu.CompilerParams(
             collective_id=1, has_side_effects=True, vmem_limit_bytes=60 * 2**20
         ),
-    )(meta, tokens, cotangent, gate5, up5, down2)
+    )(meta, tokens.T, cotangent.T, gate5, up5, down2)
 
     output, input_grad = pl.pallas_call(
         scatter_kernel,
         name="scatter_sums",
         out_shape=(
-            jax.ShapeDtypeStruct((TOK, 192), BF),
-            jax.ShapeDtypeStruct((TOK, 192), BF),
+            jax.ShapeDtypeStruct((192, TOK), BF),
+            jax.ShapeDtypeStruct((192, TOK), BF),
         ),
         in_specs=[vmem, vmem, hbm, hbm, vmem],
         out_specs=(vmem, vmem),
         scratch_shapes=[
             pltpu.VMEM((2, 24, 4, 64, 256), BF),
             pltpu.VMEM((2, 96, 256, TOK), BF),
-            pltpu.VMEM((2, 6, 7, 2, 256, TOK), BF),
-            pltpu.VMEM((2, 12, 256, TOK), BF),
+            pltpu.VMEM((2, 2, 14, 256, TOK), BF),
+            pltpu.VMEM((2, 2, 2, 12, 256, TOK), BF),
+            pltpu.VMEM((SLOTS, 6, 256, TOK), BF),
+            pltpu.VMEM((SLOTS, 6, 256, TOK), BF),
             pltpu.VMEM((2, 3, 5, 256, TOK), BF),
             pltpu.VMEM((2, 3, 64, TOK), BF),
             pltpu.VMEM((2, 2, 7, 64, TOK), BF),
@@ -861,7 +858,7 @@
             collective_id=2, has_side_effects=True, vmem_limit_bytes=60 * 2**20
         ),
     )(hid, grads, gate5, up5, wd)
-    return (output, input_grad, dgrad.reshape(1, 256, 6144))
+    return (output.T, input_grad.T, dgrad.reshape(1, 256, 6144))
 
 
 def solution(mesh):

time: 227 us -> 195 us (0.86)
  Pallas kernels: 216 us -> 186 us
  local copies, waits for them, and re-layouts: 8.61 us -> 5.27 us
    pallas_call x1, Pallas kernels: 121 us -> 84.7 us  [per_device(): pl.pallas_call(scatter_kernel, name='scatter_sums', out_shape=(jax.ShapeD...]
    pallas_call x1, Pallas kernels: 95 us -> 101 us  [per_device(): pl.pallas_call(gather_kernel, name='gather_hidden', out_shape=(jax.ShapeD...]
    unnamed x7 -> x5, local copies, waits for them, and re-layouts: 7.86 us -> 4.51 us
where the time goes in v2:
time: 195 us; the launch traced here: 193 us
  Pallas kernels  186 us (95%)
  local copies, waits for them, and re-layouts  5.27 us (3%)
    pallas_call x1, Pallas kernels, per_device(): pl.pallas_call(gather_kernel, name='gather_hidden', out_shape=(jax.ShapeD...  101 us
    pallas_call x1, Pallas kernels, per_device(): pl.pallas_call(scatter_kernel, name='scatter_sums', out_shape=(jax.ShapeD...  84.7 us
    unnamed x5, local copies, waits for them, and re-layouts  4.51 us

profile of v2, /device:TPU:8, one launch (start us, length us, event | category | flops | bytes accessed | tf_op | source)
XLA Modules:
  0.0 193.0 jit_solution(8536545851297271466)
XLA Ops:
  0.6 0.8 slice_bitcast_fusion.1
  1.4 0.8 broadcast_subtract_fusion
  2.2 0.7 select_select_fusion.meta_ref
  2.9 100.9 %gather_hidden.1 = (bf16[4,2,256,128]{3,2,1,0:T(8,128)(2,1)}, bf16[4,2,512,128]{3,2,1,0:T(8,128)(2,1)}, bf16[24,4,64,256]{3,2,1,0:T(8,128)(2,1)}, bf16[256,6144]{1,0:T(8,128)(2,1)}) custom-call(f32[8,8,128]{2,1,0:T(8,128)} %select_select_fusion.meta_ref, bf16[192,128]{1,0:T(8,128)(2,1)} %bitcast.21, bf16[192,128]{1,0:T(8,128)(2,1)} %bitcast.22, ...), custom_call_target="tpu_custom_call" | custom-call | tf_op jit(solution)/shard_map/gather_hidden/pallas_call | solution.py:802
  103.8 0.0 copy-start
  103.8 84.7 %scatter_sums.1 = (bf16[192,128]{1,0:T(8,128)(2,1)}, bf16[192,128]{1,0:T(8,128)(2,1)}) custom-call(bf16[4,2,256,128]{3,2,1,0:T(8,128)(2,1)} %get-tuple-element.9.hid_ref, bf16[4,2,512,128]{3,2,1,0:T(8,128)(2,1)} %get-tuple-element.10.grads_ref, bf16[8,4,3,64,256]{4,3,2,1,0:T(8,128)(2,1)} %bitcast.16, bf16[8,4,3,64,256]{4,3,2,1,0:T(8,128)(2,1)} %bitcast.18, ...), custom_call_target="tpu_custom_call" | custom-call | tf_op jit(solution)/shard_map/scatter_sums/pallas_call | solution.py:833
  188.5 1.4 copy.14
  189.9 1.4 copy.15
  191.3 0.0 copy-done
  191.3 1.7 copy.16
  (2 shorter events, 0.0 us)
Async XLA Ops:
  103.8 87.6 %copy-start = (bf16[256,6144]{1,0:T(8,128)(2,1)S(1)}, bf16[256,6144]{1,0:T(8,128)(2,1)}, u32[]{:S(2)}) copy-start(bf16[256,6144]{1,0:T(8,128)(2,1)} %get-tuple-element.14) | copy-start | bytes 9437188

commit v3 on v2

--- a/solution.py
+++ b/solution.py
@@ -11,7 +11,7 @@
 BF = jnp.bfloat16
 F32 = jnp.float32
 NX, NY, NZ = 4, 4, 8
-SLOTS = 6
+SLOTS = 4
 FEAT, TOK = 64, 128
 
 
@@ -119,6 +119,13 @@
     def drain(self):
         for copy in self.sent:
             copy.wait_send()
+        self.sent.clear()
+
+    def take(self, start):
+        kept, self.sent = self.sent, []
+        start()
+        taken, self.sent = self.sent, kept
+        return taken
 
 
 class Gather:
@@ -166,25 +173,47 @@
             self.copies.arrived(self.key("b1", d), b, p.at(dz=-d))
             self.copies.arrived(self.key("c1", d), c, p.at(dz=-d))
 
-    def second(self, part, d):
+    def second(self, part, rel):
         p = self.at
         if part == "a":
-            return self.buf.at[p.c, pl.ds(p.z * 4 + (p.y - d) % NY, 1)], p.at(dy=-d)
+            return self.buf.at[p.c, p.z * 4 + (p.y + rel) % NY]
         if part == "b":
-            return self.buf.at[p.c, pl.ds(32 + (p.x * 4 + (p.y - d) % NY) * 2, 2)], p.at(dy=-d)
-        return self.buf.at[p.c, pl.ds(64 + (p.y * 4 + (p.x - d) % NX) * 2, 2)], p.at(dx=-d)
+            return self.buf.at[p.c, pl.ds(32 + (p.x * 4 + (p.y + rel) % NY) * 2, 2)]
+        return self.buf.at[p.c, pl.ds(64 + (p.y * 4 + (p.x + rel) % NX) * 2, 2)]
+
+    def half(self, part, rel, sign):
+        block = self.second(part, rel)
+        if part == "a":
+            return block.at[pl.ds(0 if sign > 0 else 128, 128)]
+        return block.at[pl.ds(0 if sign > 0 else 1, 1)]
+
+    def second_to(self, part, sign):
+        return self.at.at(dx=sign) if part == "c" else self.at.at(dy=sign)
 
     def send_second(self, part):
-        p = self.at
-        block, _ = self.second(part, 0)
-        for d in range(1, 4):
-            device = p.at(dx=d) if part == "c" else p.at(dy=d)
-            self.copies.start(self.key(part + "2", d), block, block, device)
-
-    def wait_second(self, part):
-        for d in range(1, 4):
-            block, device = self.second(part, d)
-            self.copies.arrived(self.key(part + "2", d), block, device)
+        block = self.second(part, 0)
+        for sign in (1, -1):
+            self.copies.start(self.key(part + "2", sign), block, block, self.second_to(part, sign))
+
+    def second_near(self, part):
+        for sign in (-1, 1):
+            rel = -sign % 4
+            self.copies.arrived(
+                self.key(part + "2", sign), self.second(part, rel), self.second_to(part, -sign)
+            )
+            half = self.half(part, rel, sign)
+            self.copies.start(self.key(part + "2far", sign), half, half, self.second_to(part, sign))
+            self.send_own(part, (rel,))
+
+    def second_far(self, part):
+        for sign in (1, -1):
+            half = self.half(part, 2, sign)
+            self.copies.arrived(
+                self.key(part + "2far", sign), half, self.second_to(part, -sign)
+            )
+        self.send_own(part, (2,))
+        ref = self.span(part, self.at.c)
+        self.copies.start(self.key("own", part), ref, ref, self.at.at(sibling=True))
 
     def chunk(self, part, base):
         return self.buf.at[self.at.c, pl.ds(base, SIZE[part])]
@@ -209,15 +238,6 @@
             ref = self.chunk(part, self.base(part, 0, rel))
             for sign in (1, -1):
                 self.copies.start(self.key(part, sign, 1, rel), ref, ref, ring_to(self.at, part, sign))
-
-    def finish_second(self, part):
-        for rel in (1, 3, 2):
-            d = (4 - rel) % 4
-            block, device = self.second(part, d)
-            self.copies.arrived(self.key(part + "2", d), block, device)
-            self.send_own(part, (rel,))
-        ref = self.span(part, self.at.c)
-        self.copies.start(self.key("own", part), ref, ref, self.at.at(sibling=True))
 
     def messages(self, s):
         found = [("a", sign) + gather_order("a", sign)[s] for sign in (1, -1)]
@@ -293,203 +313,6 @@
                 pltpu.make_async_copy(
                     hbm.at[pl.ds(h * 4, 4), x, part], part_ref(first + x * 2 + h), sem
                 ).start()
-
-
-def gather_kernel(
-    meta_ref,
-    tok_ref,
-    cot_ref,
-    gate_hbm,
-    up_hbm,
-    down_hbm,
-    hid_ref,
-    grads_ref,
-    wd_ref,
-    dgrad_hbm,
-    tok_buf,
-    cot_buf,
-    wgu,
-    wdt,
-    flat,
-    total,
-    hgrad,
-    scaled,
-    meta,
-    wsem,
-    osem,
-    send,
-    recv,
-):
-    p = Place()
-    copies = Copies(send, recv)
-    tok = Gather("tok", p, copies, tok_buf)
-    cot = Gather("cot", p, copies, cot_buf)
-    far = [((p.seg + d) % 8, p.z * NX + p.x) for d in range(1, 8)]
-    line = [p.at(dx=d) for d in range(1, NX)] + [p.at(dz=d) for d in range(1, NZ)]
-    entered = enter(line + far)
-
-    load_blocks(gate_hbm, lambda w: wgu.at[w, 0], wsem.at[0])
-    load_blocks(up_hbm, lambda w: wgu.at[w, 1], wsem.at[0])
-    pltpu.make_async_copy(down_hbm, flat, wsem.at[1]).start()
-
-    tok.put_own(tok_ref)
-    cot.put_own(cot_ref)
-    meta[p.seg] = meta_ref[p.seg]
-    total[...] = jnp.zeros_like(total)
-    hgrad[...] = jnp.zeros_like(hgrad)
-    entered()
-
-    tok.send_first()
-    for d in range(1, 8):
-        copies.start(("meta", d), meta_ref.at[(p.seg + d) % 8], meta.at[p.seg], far[d - 1])
-
-    def turn_gu(w, carry):
-        for k in range(2):
-            block = wgu[w, k].reshape(256, 256)
-            wgu[w, k] = block.T.reshape(4, 64, 256)
-        return carry
-
-    def turn_down(i, carry):
-        block = flat[:, pl.ds(mult(i * 384, 384), 384)].T
-        z, x = i // 2, (i % 2) * 2
-        for k in range(2):
-            rows = block[k * 192 : (k + 1) * 192]
-            wd_ref[z, x + k] = rows[0:64]
-            wd_ref[8 + (x + k) * 2 + z // 4, z % 4] = rows[64:128]
-            wd_ref[16 + (x + k) * 2 + z // 4, z % 4] = rows[128:192]
-        return carry
-
-    def turn_back(w, carry):
-        wdt[w] = wd_ref[w].reshape(256, 256).T
-        return carry
-
-    def w_gu(w):
-        return wgu[w].reshape(512, 256)
-
-    def w_down(w):
-        return wdt[w]
-
-    tok.wait_first_a()
-    tok.send_own("a", (0,))
-    tok.send_second("a")
-    pltpu.make_async_copy(wgu, wgu, wsem.at[0]).wait()
-    lax.fori_loop(0, 4, turn_gu, 0)
-    tok.finish_second("a")
-    tok.wait_first_bc()
-    tok.send_own("b", (0,))
-    tok.send_own("c", (0,))
-    tok.send_second("b")
-    tok.send_second("c")
-    cot.send_first()
-    lax.fori_loop(4, 8, turn_gu, 0)
-    lax.fori_loop(8, 14, turn_gu, 0)
-    tok.finish_second("b")
-    tok.finish_second("c")
-    lax.fori_loop(14, 24, turn_gu, 0)
-    pltpu.make_async_copy(down_hbm, flat, wsem.at[1]).wait()
-
-    for s in range(14):
-        tok.ring_round(s)
-        if s == 0:
-            tok.wait_other_own()
-            tok.multiply_own(w_gu, total)
-        else:
-            tok.wait_other(s - 1)
-            tok.multiply_round(w_gu, total, s - 1)
-        if s == 2:
-            cot.wait_first_a()
-            cot.send_second("a")
-            cot.wait_first_bc()
-            cot.send_second("b")
-            cot.send_second("c")
-        if 3 <= s < 7:
-            lax.fori_loop(4 * s - 12, 4 * s - 8, turn_down, 0)
-        if 7 <= s < 10:
-            lax.fori_loop(8 * s - 56, 8 * s - 48, turn_back, 0)
-        if s == 6:
-            cot.send_own("b", (0,))
-            cot.finish_second("b")
-            cot.send_own("c", (0,))
-            cot.finish_second("c")
-        if s == 9:
-            cot.send_own("a", (0,))
-            cot.finish_second("a")
-    cot.ring_round(0)
-    tok.wait_other(13)
-    tok.multiply_round(w_gu, total, 13)
-    for d in range(1, 8):
-        copies.arrived(("meta", d), meta.at[(p.seg - d) % 8], far[7 - d])
-
-    def activate(i, carry):
-        y, r = i // 4, i % 4
-        low = mult(r * 64, 64)
-        gate = total[y, pl.ds(low, 64)]
-        upward = total[y, pl.ds(mult(256 + r * 64, 64), 64)]
-        first, second = meta[2 * y], meta[2 * y + 1]
-        share = jnp.concatenate([first[0:1], second[0:1]], axis=1)
-        scale = jnp.concatenate([first[1:2], second[1:2]], axis=1)
-        sigma = jax.nn.sigmoid(gate)
-        active = gate * sigma
-        hidden = active * upward
-        weighted = (hidden * share).astype(BF)
-        hid_ref[y, 0, pl.ds(low, 64)] = weighted[:, 0:128]
-        hid_ref[y, 1, pl.ds(low, 64)] = weighted[:, 128:256]
-        scaled[y, pl.ds(low, 64)] = (hidden * scale).astype(BF)
-        total[y, pl.ds(low, 64)] = upward * (sigma * (1.0 + gate * (1.0 - sigma))) * scale
-        total[y, pl.ds(mult(256 + r * 64, 64), 64)] = active * scale
-        return carry
-
-    lax.fori_loop(0, 16, activate, 0)
-
-    for s in range(14):
-        if s > 0:
-            cot.ring_round(s)
-        if s == 0:
-            cot.wait_other_own()
-            cot.multiply_own(w_down, hgrad)
-        else:
-            cot.wait_other(s - 1)
-            cot.multiply_round(w_down, hgrad, s - 1)
-    cot.wait_other(13)
-    cot.multiply_round(w_down, hgrad, 13)
-
-    def backward(i, carry):
-        y, r = i // 4, i % 4
-        low = mult(r * 64, 64)
-        high = mult(256 + r * 64, 64)
-        grad = hgrad[y, pl.ds(low, 64)]
-        gate_grad = (grad * total[y, pl.ds(low, 64)]).astype(BF)
-        up_grad = (grad * total[y, pl.ds(high, 64)]).astype(BF)
-        for c in range(2):
-            grads_ref[y, c, pl.ds(low, 64)] = gate_grad[:, c * 128 : (c + 1) * 128]
-            grads_ref[y, c, pl.ds(high, 64)] = up_grad[:, c * 128 : (c + 1) * 128]
-        return carry
-
-    lax.fori_loop(0, 16, backward, 0)
-
-    def weight_grad(i, carry):
-        z, x = i // 2, (i % 2) * 2
-        low = mult((z % 4) * FEAT, FEAT)
-        acc = jnp.zeros((256, 384), F32)
-        for y in range(NY):
-            halves = []
-            for c in range(2):
-                rows = []
-                for k in range(2):
-                    xk = x + k
-                    rows.append(cot_buf[c, z * 4 + y, pl.ds(mult(xk * FEAT, FEAT), FEAT), :])
-                    rows.append(cot_buf[c, 32 + (xk * 4 + y) * 2 + z // 4, pl.ds(low, FEAT), :])
-                    rows.append(cot_buf[c, 64 + (y * 4 + xk) * 2 + z // 4, pl.ds(low, FEAT), :])
-                halves.append(jnp.concatenate(rows, axis=0))
-            acc += dot_nt(scaled[y], jnp.concatenate(halves, axis=1))
-        flat[:, pl.ds(mult(i * 384, 384), 384)] = acc.astype(BF)
-        return carry
-
-    lax.fori_loop(0, 16, weight_grad, 0)
-    out = pltpu.make_async_copy(flat, dgrad_hbm, osem)
-    out.start()
-    copies.drain()
-    out.wait()
 
 
 class Scatter:
@@ -677,16 +500,28 @@
             out_ref[k * FEAT : (k + 1) * FEAT] = rows[k].astype(BF)
 
 
-def scatter_kernel(
-    hid_ref,
-    grads_ref,
+def moe_kernel(
+    meta_ref,
+    tok_ref,
+    cot_ref,
     gate_hbm,
     up_hbm,
-    wd_ref,
+    down_hbm,
     out_ref,
     in_ref,
+    dgrad_hbm,
+    tok_buf,
+    cot_buf,
     wgu,
-    pairs,
+    wd,
+    wdt,
+    flat,
+    total,
+    hgrad,
+    scaled,
+    hid,
+    grads,
+    meta,
     ring_a,
     ring_bc,
     mine,
@@ -696,56 +531,250 @@
     three_bc,
     sums,
     wsem,
+    osem,
+    free,
     send,
     recv,
+    send2,
+    recv2,
 ):
     p = Place()
     copies = Copies(send, recv)
-    entered = enter(p.others())
-    load_blocks(gate_hbm, lambda w: wgu.at[0, w], wsem.at[0])
-    load_blocks(up_hbm, lambda w: wgu.at[1, w], wsem.at[0])
+    back = Copies(send2, recv2)
+    tok = Gather("tok", p, copies, tok_buf)
+    cot = Gather("cot", p, copies, cot_buf)
+    far = [((p.seg + d) % 8, p.z * NX + p.x) for d in range(1, 8)]
+    line = [p.at(dx=d) for d in range(1, NX)] + [p.at(dz=d) for d in range(1, NZ)]
+    entered = enter(line + far)
+
+    def load_gate_up():
+        load_blocks(gate_hbm, lambda w: wgu.at[w, 0], wsem.at[0])
+        load_blocks(up_hbm, lambda w: wgu.at[w, 1], wsem.at[0])
+
+    def wait_gate_up():
+        pltpu.make_async_copy(wgu, wgu, wsem.at[0]).wait()
+
+    load_gate_up()
+    pltpu.make_async_copy(down_hbm, flat, wsem.at[1]).start()
+
+    tok.put_own(tok_ref)
+    cot.put_own(cot_ref)
+    meta[p.seg] = meta_ref[p.seg]
+    total[...] = jnp.zeros_like(total)
+    hgrad[...] = jnp.zeros_like(hgrad)
+    entered()
+
+    tok.send_first()
+    for d in range(1, 8):
+        copies.start(("meta", d), meta_ref.at[(p.seg + d) % 8], meta.at[p.seg], far[d - 1])
+
+    def turn_gu(w, carry):
+        for k in range(2):
+            block = wgu[w, k].reshape(256, 256)
+            wgu[w, k] = block.T.reshape(4, 64, 256)
+        return carry
+
+    def turn_down(i, carry):
+        block = flat[:, pl.ds(mult(i * 384, 384), 384)].T
+        z, x = i // 2, (i % 2) * 2
+        for k in range(2):
+            rows = block[k * 192 : (k + 1) * 192]
+            wd[z, x + k] = rows[0:64]
+            wd[8 + (x + k) * 2 + z // 4, z % 4] = rows[64:128]
+            wd[16 + (x + k) * 2 + z // 4, z % 4] = rows[128:192]
+        return carry
+
+    def turn_back(w, carry):
+        wdt[w] = wd[w].reshape(256, 256).T
+        return carry
+
+    def w_gu(w):
+        return wgu[w].reshape(512, 256)
+
+    def w_down(w):
+        return wdt[w]
+
+    tok.wait_first_a()
+    tok.send_second("a")
+    tok.send_own("a", (0,))
+    wait_gate_up()
+    lax.fori_loop(0, 8, turn_gu, 0)
+    tok.second_near("a")
+    tok.wait_first_bc()
+    for part in ("b", "c"):
+        tok.send_second(part)
+        tok.send_own(part, (0,))
+    tok.second_far("a")
+    cot.send_first()
+    lax.fori_loop(8, 24, turn_gu, 0)
+    tok.second_near("b")
+    tok.second_near("c")
+    pltpu.make_async_copy(down_hbm, flat, wsem.at[1]).wait()
+    tok.second_far("b")
+    tok.second_far("c")
+
+    for s in range(14):
+        tok.ring_round(s)
+        if s == 0:
+            tok.wait_other_own()
+            tok.multiply_own(w_gu, total)
+        else:
+            tok.wait_other(s - 1)
+            tok.multiply_round(w_gu, total, s - 1)
+        if s == 1:
+            cot.wait_first_a()
+            cot.send_second("a")
+        if s == 2:
+            cot.wait_first_bc()
+            cot.send_second("b")
+            cot.send_second("c")
+        if 3 <= s < 7:
+            lax.fori_loop(4 * s - 12, 4 * s - 8, turn_down, 0)
+        if s == 6:
+            cot.send_own("b", (0,))
+            cot.second_near("b")
+            cot.send_own("c", (0,))
+            cot.second_near("c")
+        if 7 <= s < 10:
+            lax.fori_loop(8 * s - 56, 8 * s - 48, turn_back, 0)
+        if s == 8:
+            cot.second_far("b")
+            cot.second_far("c")
+        if s == 9:
+            cot.send_own("a", (0,))
+            cot.second_near("a")
+        if s == 10:
+            cot.second_far("a")
+    cot.ring_round(0)
+    tok.wait_other(13)
+    tok.multiply_round(w_gu, total, 13)
+    load_gate_up()
+    for d in range(1, 8):
+        copies.arrived(("meta", d), meta.at[(p.seg - d) % 8], far[7 - d])
+
+    def activate(i, carry):
+        y, r = i // 4, i % 4
+        low = mult(r * 64, 64)
+        gate = total[y, pl.ds(low, 64)]
+        upward = total[y, pl.ds(mult(256 + r * 64, 64), 64)]
+        first, second = meta[2 * y], meta[2 * y + 1]
+        share = jnp.concatenate([first[0:1], second[0:1]], axis=1)
+        scale = jnp.concatenate([first[1:2], second[1:2]], axis=1)
+        sigma = jax.nn.sigmoid(gate)
+        active = gate * sigma
+        hidden = active * upward
+        weighted = (hidden * share).astype(BF)
+        hid[y, 0, pl.ds(low, 64)] = weighted[:, 0:128]
+        hid[y, 1, pl.ds(low, 64)] = weighted[:, 128:256]
+        scaled[y, pl.ds(low, 64)] = (hidden * scale).astype(BF)
+        total[y, pl.ds(low, 64)] = upward * (sigma * (1.0 + gate * (1.0 - sigma))) * scale
+        total[y, pl.ds(mult(256 + r * 64, 64), 64)] = active * scale
+        return carry
+
+    lax.fori_loop(0, 16, activate, 0)
+
+    pairs = tok_buf
+
+    def lhs_in(w):
+        return jnp.concatenate(
+            [wgu[w, 0].reshape(256, 256), wgu[w, 1].reshape(256, 256)], axis=1
+        )
 
     def bufs(i):
         return (two.at[i], three_a.at[i], three_bc.at[i], sums.at[i])
 
-    def lhs_in(w):
-        return jnp.concatenate(
-            [wgu[0, w].reshape(256, 256), wgu[1, w].reshape(256, 256)], axis=1
-        )
-
     out = Scatter(
-        "out", 0, p, copies, lambda w: wd_ref[w].reshape(256, 256), lambda y, c: hid_ref[y, c],
+        "out", 0, p, back, lambda w: wd[w].reshape(256, 256), lambda y, c: hid[y, c],
         pairs.at[0], ring_a.at[0], ring_bc.at[0], mine, stage, bufs(0),
     )
     inp = Scatter(
-        "in", 16, p, copies, lhs_in, lambda y, c: grads_ref[y, c],
+        "in", 16, p, back, lhs_in, lambda y, c: grads[y, c],
         pairs.at[1], ring_a.at[1], ring_bc.at[1], mine, stage, bufs(1),
     )
-    entered()
-
-    steps = [(out, j) for j in range(16)] + [(inp, j) for j in range(16)]
     sent = []
 
     def produce(n):
-        which, j = steps[n]
+        which, j = (out, n) if n < 16 else (inp, n - 16)
         if n >= SLOTS:
             for copy in sent[n - SLOTS]:
                 copy.wait_send()
-        before = len(copies.sent)
-        which.produce(j)
-        sent.append(copies.sent[before:])
-        del copies.sent[before:]
-
-    for n in range(2):
-        produce(n)
+        sent.append(back.take(lambda: which.produce(j)))
+
     for s in range(14):
+        if s > 0:
+            cot.ring_round(s)
+        if s == 0:
+            cot.wait_other_own()
+            cot.multiply_own(w_down, hgrad)
+        else:
+            cot.wait_other(s - 1)
+            cot.multiply_round(w_down, hgrad, s - 1)
+        if s == 9:
+            copies.drain()
+            pl.semaphore_signal(
+                free, inc=1, device_id=p.at(sibling=True), device_id_type=MESH
+            )
+        if s == 10:
+            pl.semaphore_wait(free, 1)
+            produce(0)
+        if s == 11:
+            produce(1)
+            out.send_round(0)
+        if s == 12:
+            produce(2)
+            out.send_round(1)
+        if s == 13:
+            produce(3)
+            out.send_round(2)
+    cot.wait_other(13)
+    cot.multiply_round(w_down, hgrad, 13)
+
+    def backward(i, carry):
+        y, r = i // 4, i % 4
+        low = mult(r * 64, 64)
+        high = mult(256 + r * 64, 64)
+        grad = hgrad[y, pl.ds(low, 64)]
+        gate_grad = (grad * total[y, pl.ds(low, 64)]).astype(BF)
+        up_grad = (grad * total[y, pl.ds(high, 64)]).astype(BF)
+        for c in range(2):
+            grads[y, c, pl.ds(low, 64)] = gate_grad[:, c * 128 : (c + 1) * 128]
+            grads[y, c, pl.ds(high, 64)] = up_grad[:, c * 128 : (c + 1) * 128]
+        return carry
+
+    lax.fori_loop(0, 16, backward, 0)
+
+    def weight_grad(i, carry):
+        z, x = i // 2, (i % 2) * 2
+        low = mult((z % 4) * FEAT, FEAT)
+        acc = jnp.zeros((256, 384), F32)
+        for y in range(NY):
+            halves = []
+            for c in range(2):
+                rows = []
+                for k in range(2):
+                    xk = x + k
+                    rows.append(cot_buf[c, z * 4 + y, pl.ds(mult(xk * FEAT, FEAT), FEAT), :])
+                    rows.append(cot_buf[c, 32 + (xk * 4 + y) * 2 + z // 4, pl.ds(low, FEAT), :])
+                    rows.append(cot_buf[c, 64 + (y * 4 + xk) * 2 + z // 4, pl.ds(low, FEAT), :])
+                halves.append(jnp.concatenate(rows, axis=0))
+            acc += dot_nt(scaled[y], jnp.concatenate(halves, axis=1))
+        flat[:, pl.ds(mult(i * 384, 384), 384)] = acc.astype(BF)
+        return carry
+
+    produce(4)
+    for s in range(3, 14):
         out.send_round(s)
         produce(s + 2)
+        if s in (4, 6, 8, 10):
+            lax.fori_loop(2 * s - 8, 2 * s - 4, weight_grad, 0)
+        if s == 10:
+            dgrad = pltpu.make_async_copy(flat, dgrad_hbm, osem)
+            dgrad.start()
         if s == 12:
             out.finish_ring("b", (1, 2))
         if s == 13:
             out.finish_ring("c", (1, 2))
-    pltpu.make_async_copy(wgu, wgu, wsem.at[0]).wait()
+    wait_gate_up()
     produce(16)
     inp.send_round(0)
     produce(17)
@@ -778,6 +807,8 @@
         for copy in group:
             copy.wait_send()
     copies.drain()
+    back.drain()
+    dgrad.wait()
 
 
 def per_device(
@@ -799,49 +830,29 @@
     hbm = pl.BlockSpec(memory_space=pl.ANY)
     n_gather, n_scatter = 288, 288
 
-    hid, grads, wd, dgrad = pl.pallas_call(
-        gather_kernel,
-        name="gather_hidden",
+    output, input_grad, dgrad = pl.pallas_call(
+        moe_kernel,
+        name="moe",
         out_shape=(
-            jax.ShapeDtypeStruct((NY, 2, 256, TOK), BF),
-            jax.ShapeDtypeStruct((NY, 2, 512, TOK), BF),
-            jax.ShapeDtypeStruct((24, 4, 64, 256), BF),
+            jax.ShapeDtypeStruct((192, TOK), BF),
+            jax.ShapeDtypeStruct((192, TOK), BF),
             jax.ShapeDtypeStruct((256, 6144), BF),
         ),
         in_specs=[vmem, vmem, vmem, hbm, hbm, hbm],
-        out_specs=(vmem, vmem, vmem, hbm),
+        out_specs=(vmem, vmem, hbm),
         scratch_shapes=[
             pltpu.VMEM((2, 96, 256, TOK), BF),
             pltpu.VMEM((2, 96, 256, TOK), BF),
             pltpu.VMEM((24, 2, 4, 64, 256), BF),
+            pltpu.VMEM((24, 4, 64, 256), BF),
             pltpu.VMEM((24, 256, 256), BF),
             pltpu.VMEM((256, 6144), BF),
             pltpu.VMEM((NY, 512, 256), F32),
             pltpu.VMEM((NY, 256, 256), F32),
             pltpu.VMEM((NY, 256, 256), BF),
+            pltpu.VMEM((NY, 2, 256, TOK), BF),
+            pltpu.VMEM((NY, 2, 512, TOK), BF),
             pltpu.VMEM((8, 8, TOK), F32),
-            pltpu.SemaphoreType.DMA((2,)),
-            pltpu.SemaphoreType.DMA,
-            pltpu.SemaphoreType.DMA((n_gather,)),
-            pltpu.SemaphoreType.DMA((n_gather,)),
-        ],
-        compiler_params=pltpu.CompilerParams(
-            collective_id=1, has_side_effects=True, vmem_limit_bytes=60 * 2**20
-        ),
-    )(meta, tokens.T, cotangent.T, gate5, up5, down2)
-
-    output, input_grad = pl.pallas_call(
-        scatter_kernel,
-        name="scatter_sums",
-        out_shape=(
-            jax.ShapeDtypeStruct((192, TOK), BF),
-            jax.ShapeDtypeStruct((192, TOK), BF),
-        ),
-        in_specs=[vmem, vmem, hbm, hbm, vmem],
-        out_specs=(vmem, vmem),
-        scratch_shapes=[
-            pltpu.VMEM((2, 24, 4, 64, 256), BF),
-            pltpu.VMEM((2, 96, 256, TOK), BF),
             pltpu.VMEM((2, 2, 14, 256, TOK), BF),
             pltpu.VMEM((2, 2, 2, 12, 256, TOK), BF),
             pltpu.VMEM((SLOTS, 6, 256, TOK), BF),
@@ -850,14 +861,18 @@
             pltpu.VMEM((2, 3, 64, TOK), BF),
             pltpu.VMEM((2, 2, 7, 64, TOK), BF),
             pltpu.VMEM((2, 5, 4, 64, TOK), BF),
-            pltpu.SemaphoreType.DMA((1,)),
+            pltpu.SemaphoreType.DMA((2,)),
+            pltpu.SemaphoreType.DMA,
+            pltpu.SemaphoreType.REGULAR,
+            pltpu.SemaphoreType.DMA((n_gather,)),
+            pltpu.SemaphoreType.DMA((n_gather,)),
             pltpu.SemaphoreType.DMA((n_scatter,)),
             pltpu.SemaphoreType.DMA((n_scatter,)),
         ],
         compiler_params=pltpu.CompilerParams(
-            collective_id=2, has_side_effects=True, vmem_limit_bytes=60 * 2**20
+            collective_id=1, has_side_effects=True, vmem_limit_bytes=62 * 2**20
         ),
-    )(hid, grads, gate5, up5, wd)
+    )(meta, tokens.T, cotangent.T, gate5, up5, down2)
     return (output.T, input_grad.T, dgrad.reshape(1, 256, 6144))
 
 

time: 195 us -> 185 us (0.949)
  Pallas kernels: 186 us -> 175 us
  local copies, waits for them, and re-layouts: 5.27 us -> 7.48 us
    pallas_call x2 -> x1, Pallas kernels: 186 us -> 175 us  [per_device(): pl.pallas_call(moe_kernel, name='moe', out_shape=(jax.ShapeDtypeStruct((1...]
    unnamed x5 -> x3, local copies, waits for them, and re-layouts: 4.51 us -> 6.72 us
where the time goes in v3:
time: 185 us
  Pallas kernels  175 us (95%)
  local copies, waits for them, and re-layouts  7.48 us (4%)
    pallas_call x1, Pallas kernels, per_device(): pl.pallas_call(moe_kernel, name='moe', out_shape=(jax.ShapeDtypeStruct((1...  175 us
    unnamed x3, local copies, waits for them, and re-layouts  6.72 us

profile of v3, /device:TPU:8, one launch (start us, length us, event | category | flops | bytes accessed | tf_op | source)
XLA Modules:
  0.0 184.8 jit_solution(5308649319291953207)
XLA Ops:
  0.6 0.8 slice_bitcast_fusion.1
  1.4 0.8 broadcast_subtract_fusion
  2.2 0.7 select_select_fusion.meta_ref
  2.9 175.2 %moe.1 = (bf16[192,128]{1,0:T(8,128)(2,1)}, bf16[192,128]{1,0:T(8,128)(2,1)}, bf16[256,6144]{1,0:T(8,128)(2,1)}) custom-call(f32[8,8,128]{2,1,0:T(8,128)} %select_select_fusion.meta_ref, bf16[192,128]{1,0:T(8,128)(2,1)} %bitcast.19, bf16[192,128]{1,0:T(8,128)(2,1)} %bitcast.20, bf16[8,4,3,64,256]{4,3,2,1,0:T(8,128)(2,1)} %bitcast.16, ...), custom_call_target="tpu_custom_call" | custom-call | tf_op jit(solution)/shard_map/moe/pallas_call | solution.py:833
  178.0 1.4 copy.14
  179.5 1.4 copy.15
  180.9 3.9 %copy.16 = bf16[1,256,6144]{2,1,0:T(8,128)(2,1)} copy(bf16[1,256,6144]{2,1,0:T(8,128)(2,1)} %bitcast.15) | data formatting | bytes 6291456
  (2 shorter events, 0.0 us)

commit v4 on v3

--- a/solution.py
+++ b/solution.py
@@ -239,15 +239,17 @@
             for sign in (1, -1):
                 self.copies.start(self.key(part, sign, 1, rel), ref, ref, ring_to(self.at, part, sign))
 
-    def messages(self, s):
-        found = [("a", sign) + gather_order("a", sign)[s] for sign in (1, -1)]
-        part, n = ("b", "c")[s % 2], s // 2
-        if n < 6:
-            found += [(part, sign) + gather_order(part, sign)[n] for sign in (1, -1)]
+    def messages(self, s, u):
+        found = []
+        if 0 <= s < 14:
+            found += [("a", sign) + gather_order("a", sign)[s] for sign in (1, -1)]
+        if 0 <= u < 12:
+            part = ("b", "c")[u % 2]
+            found += [(part, sign) + gather_order(part, sign)[u // 2] for sign in (1, -1)]
         return found
 
-    def ring_round(self, s):
-        for part, sign, hop, rel in self.messages(s):
+    def ring_round(self, s, u):
+        for part, sign, hop, rel in self.messages(s, u):
             ref = self.chunk(part, self.base(part, sign * hop, rel))
             self.copies.arrived(self.key(part, sign, hop, rel), ref, ring_to(self.at, part, -sign))
             if (hop + 1, rel) in gather_order(part, sign):
@@ -258,9 +260,9 @@
                 self.key("sib", part, sign, hop, rel), ref, ref, self.at.at(sibling=True)
             )
 
-    def wait_other(self, s):
-        p = self.at
-        for part, sign, hop, rel in self.messages(s):
+    def wait_other(self, s, u):
+        p = self.at
+        for part, sign, hop, rel in self.messages(s, u):
             ref = self.buf.at[1 - p.c, pl.ds(self.base(part, sign * hop, rel), SIZE[part])]
             self.copies.arrived(self.key("sib", part, sign, hop, rel), ref, p.at(sibling=True))
 
@@ -292,13 +294,17 @@
 
         lax.fori_loop(0, 4, step, 0)
 
-    def multiply_round(self, weights, total, s):
-        bases = [self.base(part, sign * hop, rel) for part, sign, hop, rel in self.messages(s)]
+    def multiply_round(self, weights, total, s, u):
+        messages = self.messages(s, u)
+        bases = [self.base(part, sign * hop, rel) for part, sign, hop, rel in messages]
+        if not bases:
+            return
 
         def step(t, carry):
-            self.multiply_single(weights, total, jnp.where(t == 0, bases[0], bases[1]))
-            if len(bases) > 2:
-                self.multiply_chunk(weights, total, jnp.where(t == 0, bases[2], bases[3]))
+            if messages[0][0] == "a":
+                self.multiply_single(weights, total, jnp.where(t == 0, bases[0], bases[1]))
+            if messages[-1][0] != "a":
+                self.multiply_chunk(weights, total, jnp.where(t == 0, bases[-2], bases[-1]))
             return carry
 
         lax.fori_loop(0, 2, step, 0)
@@ -335,32 +341,25 @@
             return 32 + (((p.x + ahead) % NX) * 4 + (p.y + rel) % NY) * 2
         return 64 + (((p.y + ahead) % NY) * 4 + (p.x + rel) % NX) * 2
 
-    def chunks(self, j):
-        found = []
-        for i, sign in enumerate((1, -1)):
-            if j < 14:
-                found.append(("a", sign) + scatter_order("a", sign)[j])
-            else:
-                found.append(("a", 0, 0, ((1, 2), (3, 0))[j - 14][i]))
-        part, n = ("b", "c")[j % 2], j // 2
-        for i, sign in enumerate((1, -1)):
-            if n < 6:
-                found.append((part, sign) + scatter_order(part, sign)[n])
-            else:
-                found.append((part, 0, 0, ((1, 2), (3, 0))[n - 6][i]))
-        return found
+    def chunks(self, kind, j):
+        part, n = ("a", j) if kind == "a" else (("b", "c")[j % 2], j // 2)
+        count = 14 if kind == "a" else 6
+        if n < count:
+            return [(part, sign) + scatter_order(part, sign)[n] for sign in (1, -1)]
+        return [(part, 0, 0, rel) for rel in ((1, 2), (3, 0))[n - count]]
 
     def place_of(self, chunk):
+        kind = "a" if chunk[0] == "a" else "bc"
         for j in range(16):
-            chunks = self.chunks(j)
+            chunks = self.chunks(kind, j)
             if chunk in chunks:
                 k = chunks.index(chunk)
-                return (self.first + j) % SLOTS, (0, 1, 2, 4)[k]
-
-    def produce(self, j):
+                return (self.first + j) % SLOTS, (k if kind == "a" else 2 + 2 * k)
+
+    def produce(self, kind, j):
         p = self.at
         slot = (self.first + j) % SLOTS
-        chunks = self.chunks(j)
+        chunks = self.chunks(kind, j)
         bases = [self.base(part, sign * hop, rel) for part, sign, hop, rel in chunks]
 
         def one(w, rhs, at):
@@ -373,11 +372,12 @@
 
         def step(t, carry):
             b = jnp.where(t == 0, bases[0], bases[1])
-            one(b // 4, rhs_of(b % 4), t)
-            b = jnp.where(t == 0, bases[2], bases[3])
-            w, rhs = weight_of(b), rhs_of(row_of(b))
-            one(w, rhs, 2 + 2 * t)
-            one(w + 1, rhs, 3 + 2 * t)
+            if kind == "a":
+                one(b // 4, rhs_of(b % 4), t)
+            else:
+                w, rhs = weight_of(b), rhs_of(row_of(b))
+                one(w, rhs, 2 + 2 * t)
+                one(w + 1, rhs, 3 + 2 * t)
             return carry
 
         lax.fori_loop(0, 2, step, 0)
@@ -416,8 +416,8 @@
             self.pairs[base + t] = value.astype(BF)
         return ref
 
-    def send_round(self, s):
-        for chunk in self.chunks(s):
+    def send_round(self, kind, j):
+        for chunk in self.chunks(kind, j):
             part, sign, hop, rel = chunk
             if sign == 0:
                 continue
@@ -450,54 +450,55 @@
             return pl.ds(32 + (p.x * 4 + (p.y + d) % NY) * 2, 2), pl.ds(1, 2), p.at(dy=d)
         return pl.ds(64 + (p.y * 4 + (p.x + d) % NX) * 2, 2), pl.ds(3, 2), p.at(dx=d)
 
-    def sum_second(self):
-        p = self.at
-        for part, slots in (("a", (0,)), ("b", (1, 2)), ("c", (3, 4))):
-            for d in range(1, 4):
-                _, slot, _ = self.second(part, d)
-                device = p.at(dx=-d) if part == "c" else p.at(dy=-d)
-                self.copies.arrived(self.key(part + "2", d), self.two.at[d - 1, slot], device)
-            for t, slot in enumerate(slots):
-                mine = {
-                    "a": p.z * 4 + p.y,
-                    "b": 32 + (p.x * 4 + p.y) * 2 + t,
-                    "c": 64 + (p.y * 4 + p.x) * 2 + t,
-                }[part]
-                value = self.pairs[mine].astype(F32)
-                for d in range(3):
-                    value += self.two[d, slot].astype(F32)
-                self.sums[slot] = value.astype(BF).reshape(4, 64, TOK)
-        for d in range(1, NX):
-            x = (p.x + d) % NX
-            self.copies.start(
-                self.key("a3", d), self.sums.at[0, x], self.three_a.at[d - 1], p.at(dx=d)
-            )
+    def sum_second(self, part):
+        p = self.at
+        slots = {"a": (0,), "b": (1, 2), "c": (3, 4)}[part]
+        for d in range(1, 4):
+            _, slot, _ = self.second(part, d)
+            device = p.at(dx=-d) if part == "c" else p.at(dy=-d)
+            self.copies.arrived(self.key(part + "2", d), self.two.at[d - 1, slot], device)
+        for t, slot in enumerate(slots):
+            mine = {
+                "a": p.z * 4 + p.y,
+                "b": 32 + (p.x * 4 + p.y) * 2 + t,
+                "c": 64 + (p.y * 4 + p.x) * 2 + t,
+            }[part]
+            value = self.pairs[mine].astype(F32)
+            for d in range(3):
+                value += self.two[d, slot].astype(F32)
+            self.sums[slot] = value.astype(BF).reshape(4, 64, TOK)
+        if part == "a":
+            for d in range(1, NX):
+                x = (p.x + d) % NX
+                self.copies.start(
+                    self.key("a3", d), self.sums.at[0, x], self.three_a.at[d - 1], p.at(dx=d)
+                )
+            return
+        first, i = {"b": (1, 0), "c": (3, 1)}[part]
         for d in range(1, NZ):
             z = (p.z + d) % NZ
-            for part, first, i in (("b", 1, 0), ("c", 3, 1)):
-                self.copies.start(
-                    self.key(part + "3", d),
-                    self.sums.at[first + z // 4, z % 4],
-                    self.three_bc.at[i, d - 1],
-                    p.at(dz=d),
-                )
-
-    def sum_third(self, out_ref):
-        p = self.at
-        rows = [self.sums[0, p.x].astype(F32)]
-        for d in range(1, NX):
-            self.copies.arrived(self.key("a3", d), self.three_a.at[d - 1], p.at(dx=-d))
-            rows[0] += self.three_a[d - 1].astype(F32)
-        for part, first, i in (("b", 1, 0), ("c", 3, 1)):
-            value = self.sums[first + p.z // 4, p.z % 4].astype(F32)
-            for d in range(1, NZ):
-                self.copies.arrived(
-                    self.key(part + "3", d), self.three_bc.at[i, d - 1], p.at(dz=-d)
-                )
-                value += self.three_bc[i, d - 1].astype(F32)
-            rows.append(value)
-        for k in range(3):
-            out_ref[k * FEAT : (k + 1) * FEAT] = rows[k].astype(BF)
+            self.copies.start(
+                self.key(part + "3", d),
+                self.sums.at[first + z // 4, z % 4],
+                self.three_bc.at[i, d - 1],
+                p.at(dz=d),
+            )
+
+    def sum_third(self, part, out_ref):
+        p = self.at
+        if part == "a":
+            value = self.sums[0, p.x].astype(F32)
+            for d in range(1, NX):
+                self.copies.arrived(self.key("a3", d), self.three_a.at[d - 1], p.at(dx=-d))
+                value += self.three_a[d - 1].astype(F32)
+            out_ref[0:FEAT] = value.astype(BF)
+            return
+        first, i = {"b": (1, 0), "c": (3, 1)}[part]
+        value = self.sums[first + p.z // 4, p.z % 4].astype(F32)
+        for d in range(1, NZ):
+            self.copies.arrived(self.key(part + "3", d), self.three_bc.at[i, d - 1], p.at(dz=-d))
+            value += self.three_bc[i, d - 1].astype(F32)
+        out_ref[(i + 1) * FEAT : (i + 2) * FEAT] = value.astype(BF)
 
 
 def moe_kernel(
@@ -594,64 +595,6 @@
     def w_down(w):
         return wdt[w]
 
-    tok.wait_first_a()
-    tok.send_second("a")
-    tok.send_own("a", (0,))
-    wait_gate_up()
-    lax.fori_loop(0, 8, turn_gu, 0)
-    tok.second_near("a")
-    tok.wait_first_bc()
-    for part in ("b", "c"):
-        tok.send_second(part)
-        tok.send_own(part, (0,))
-    tok.second_far("a")
-    cot.send_first()
-    lax.fori_loop(8, 24, turn_gu, 0)
-    tok.second_near("b")
-    tok.second_near("c")
-    pltpu.make_async_copy(down_hbm, flat, wsem.at[1]).wait()
-    tok.second_far("b")
-    tok.second_far("c")
-
-    for s in range(14):
-        tok.ring_round(s)
-        if s == 0:
-            tok.wait_other_own()
-            tok.multiply_own(w_gu, total)
-        else:
-            tok.wait_other(s - 1)
-            tok.multiply_round(w_gu, total, s - 1)
-        if s == 1:
-            cot.wait_first_a()
-            cot.send_second("a")
-        if s == 2:
-            cot.wait_first_bc()
-            cot.send_second("b")
-            cot.send_second("c")
-        if 3 <= s < 7:
-            lax.fori_loop(4 * s - 12, 4 * s - 8, turn_down, 0)
-        if s == 6:
-            cot.send_own("b", (0,))
-            cot.second_near("b")
-            cot.send_own("c", (0,))
-            cot.second_near("c")
-        if 7 <= s < 10:
-            lax.fori_loop(8 * s - 56, 8 * s - 48, turn_back, 0)
-        if s == 8:
-            cot.second_far("b")
-            cot.second_far("c")
-        if s == 9:
-            cot.send_own("a", (0,))
-            cot.second_near("a")
-        if s == 10:
-            cot.second_far("a")
-    cot.ring_round(0)
-    tok.wait_other(13)
-    tok.multiply_round(w_gu, total, 13)
-    load_gate_up()
-    for d in range(1, 8):
-        copies.arrived(("meta", d), meta.at[(p.seg - d) % 8], far[7 - d])
-
     def activate(i, carry):
         y, r = i // 4, i % 4
         low = mult(r * 64, 64)
@@ -671,64 +614,6 @@
         total[y, pl.ds(mult(256 + r * 64, 64), 64)] = active * scale
         return carry
 
-    lax.fori_loop(0, 16, activate, 0)
-
-    pairs = tok_buf
-
-    def lhs_in(w):
-        return jnp.concatenate(
-            [wgu[w, 0].reshape(256, 256), wgu[w, 1].reshape(256, 256)], axis=1
-        )
-
-    def bufs(i):
-        return (two.at[i], three_a.at[i], three_bc.at[i], sums.at[i])
-
-    out = Scatter(
-        "out", 0, p, back, lambda w: wd[w].reshape(256, 256), lambda y, c: hid[y, c],
-        pairs.at[0], ring_a.at[0], ring_bc.at[0], mine, stage, bufs(0),
-    )
-    inp = Scatter(
-        "in", 16, p, back, lhs_in, lambda y, c: grads[y, c],
-        pairs.at[1], ring_a.at[1], ring_bc.at[1], mine, stage, bufs(1),
-    )
-    sent = []
-
-    def produce(n):
-        which, j = (out, n) if n < 16 else (inp, n - 16)
-        if n >= SLOTS:
-            for copy in sent[n - SLOTS]:
-                copy.wait_send()
-        sent.append(back.take(lambda: which.produce(j)))
-
-    for s in range(14):
-        if s > 0:
-            cot.ring_round(s)
-        if s == 0:
-            cot.wait_other_own()
-            cot.multiply_own(w_down, hgrad)
-        else:
-            cot.wait_other(s - 1)
-            cot.multiply_round(w_down, hgrad, s - 1)
-        if s == 9:
-            copies.drain()
-            pl.semaphore_signal(
-                free, inc=1, device_id=p.at(sibling=True), device_id_type=MESH
-            )
-        if s == 10:
-            pl.semaphore_wait(free, 1)
-            produce(0)
-        if s == 11:
-            produce(1)
-            out.send_round(0)
-        if s == 12:
-            produce(2)
-            out.send_round(1)
-        if s == 13:
-            produce(3)
-            out.send_round(2)
-    cot.wait_other(13)
-    cot.multiply_round(w_down, hgrad, 13)
-
     def backward(i, carry):
         y, r = i // 4, i % 4
         low = mult(r * 64, 64)
@@ -740,8 +625,6 @@
             grads[y, c, pl.ds(low, 64)] = gate_grad[:, c * 128 : (c + 1) * 128]
             grads[y, c, pl.ds(high, 64)] = up_grad[:, c * 128 : (c + 1) * 128]
         return carry
-
-    lax.fori_loop(0, 16, backward, 0)
 
     def weight_grad(i, carry):
         z, x = i // 2, (i % 2) * 2
@@ -761,51 +644,166 @@
         flat[:, pl.ds(mult(i * 384, 384), 384)] = acc.astype(BF)
         return carry
 
-    produce(4)
-    for s in range(3, 14):
-        out.send_round(s)
-        produce(s + 2)
-        if s in (4, 6, 8, 10):
-            lax.fori_loop(2 * s - 8, 2 * s - 4, weight_grad, 0)
-        if s == 10:
+    pairs = tok_buf
+
+    def lhs_in(w):
+        return jnp.concatenate(
+            [wgu[w, 0].reshape(256, 256), wgu[w, 1].reshape(256, 256)], axis=1
+        )
+
+    def bufs(i):
+        return (two.at[i], three_a.at[i], three_bc.at[i], sums.at[i])
+
+    out = Scatter(
+        "out", 0, p, back, lambda w: wd[w].reshape(256, 256), lambda y, c: hid[y, c],
+        pairs.at[0], ring_a.at[0], ring_bc.at[0], mine, stage, bufs(0),
+    )
+    inp = Scatter(
+        "in", 16, p, back, lhs_in, lambda y, c: grads[y, c],
+        pairs.at[1], ring_a.at[1], ring_bc.at[1], mine, stage, bufs(1),
+    )
+    sent = {"a": [], "bc": []}
+
+    def step_of(n):
+        return (out, n) if n < 16 else (inp, n - 16)
+
+    def produce(kind, n):
+        if not 0 <= n < 32:
+            return
+        which, j = step_of(n)
+        if n >= SLOTS:
+            for copy in sent[kind][n - SLOTS]:
+                copy.wait_send()
+        sent[kind].append(back.take(lambda: which.produce(kind, j)))
+
+    def turn(kind, n):
+        if not 0 <= n < 32:
+            return
+        which, j = step_of(n)
+        if kind == "a":
+            if j < 14:
+                which.send_round("a", j)
+            else:
+                which.finish_ring("a", ((1, 2), (3, 0))[j - 14])
+        elif j < 12:
+            which.send_round("bc", j)
+        else:
+            which.finish_ring(("b", "c")[j % 2], ((1, 2), (3, 0))[(j - 12) // 2])
+
+    tok.wait_first_a()
+    tok.send_second("a")
+    tok.send_own("a", (0,))
+    wait_gate_up()
+    lax.fori_loop(0, 8, turn_gu, 0)
+    tok.second_near("a")
+    tok.wait_first_bc()
+    for part in ("b", "c"):
+        tok.send_second(part)
+        tok.send_own(part, (0,))
+    tok.second_far("a")
+    lax.fori_loop(8, 16, turn_gu, 0)
+
+    lag, first_bc, first_a = 4, 23, 27
+    for n in range(first_a + 32):
+        if n < 14:
+            tok.ring_round(n, -1)
+        elif n < 28:
+            cot.ring_round(n - 14, -1)
+        if lag <= n < 12 + lag:
+            tok.ring_round(-1, n - lag)
+        elif 12 + lag <= n < 24 + lag:
+            cot.ring_round(-1, n - 12 - lag)
+        if n == 0:
+            lax.fori_loop(16, 24, turn_gu, 0)
+        if n == 1:
+            tok.second_near("b")
+        if n == 2:
+            tok.second_near("c")
+            cot.send_first()
+        if n == 3:
+            tok.second_far("b")
+            tok.second_far("c")
+            pltpu.make_async_copy(down_hbm, flat, wsem.at[1]).wait()
+        if n == 4:
+            tok.wait_other_own()
+            tok.multiply_own(w_gu, total)
+        if 1 <= n <= 16:
+            k = n - 1
+            tok.wait_other(k, k - lag)
+            tok.multiply_round(w_gu, total, k, k - lag)
+        if 5 <= n < 9:
+            lax.fori_loop(4 * n - 20, 4 * n - 16, turn_down, 0)
+        if 9 <= n < 13:
+            lax.fori_loop(6 * n - 54, 6 * n - 48, turn_back, 0)
+        if n == 7:
+            cot.wait_first_a()
+            cot.send_second("a")
+            cot.wait_first_bc()
+            cot.send_second("b")
+            cot.send_second("c")
+        if n == 10:
+            cot.send_own("b", (0,))
+            cot.second_near("b")
+            cot.send_own("c", (0,))
+            cot.second_near("c")
+            cot.send_own("a", (0,))
+            cot.second_near("a")
+        if n == 11:
+            cot.second_far("a")
+        if n == 12:
+            cot.second_far("b")
+            cot.second_far("c")
+        if n == 16:
+            before, copies.sent = copies.sent, []
+            load_gate_up()
+            for d in range(1, 8):
+                copies.arrived(("meta", d), meta.at[(p.seg - d) % 8], far[7 - d])
+            lax.fori_loop(0, 16, activate, 0)
+        if n == 17:
+            cot.wait_other_own()
+            cot.multiply_own(w_down, hgrad)
+        if 15 <= n <= 28:
+            k = n - 1
+            cot.wait_other(k - 14, k - 12 - lag)
+            cot.multiply_round(w_down, hgrad, k - 14, k - 12 - lag)
+        if n == 20:
+            for copy in before:
+                copy.wait_send()
+            pl.semaphore_signal(
+                free, inc=1, device_id=p.at(sibling=True), device_id_type=MESH
+            )
+        if n == 21:
+            pl.semaphore_wait(free, 1)
+        if n == 28:
+            lax.fori_loop(0, 16, backward, 0)
+        if 29 <= n < 37:
+            lax.fori_loop(2 * n - 58, 2 * n - 56, weight_grad, 0)
+        if n == 37:
             dgrad = pltpu.make_async_copy(flat, dgrad_hbm, osem)
             dgrad.start()
-        if s == 12:
-            out.finish_ring("b", (1, 2))
-        if s == 13:
-            out.finish_ring("c", (1, 2))
-    wait_gate_up()
-    produce(16)
-    inp.send_round(0)
-    produce(17)
-    inp.send_round(1)
-    out.finish_ring("a", (1, 2))
-    out.finish_ring("b", (3, 0))
-    produce(18)
-    inp.send_round(2)
-    out.finish_ring("a", (3, 0))
-    out.finish_ring("c", (3, 0))
-    produce(19)
-    for s in range(3, 14):
-        inp.send_round(s)
-        produce(s + 17)
-        if s == 4:
-            out.sum_second()
-        if s == 7:
-            out.sum_third(out_ref)
-        if s == 12:
-            inp.finish_ring("b", (1, 2))
-        if s == 13:
-            inp.finish_ring("c", (1, 2))
-    produce(31)
-    inp.finish_ring("b", (3, 0))
-    inp.finish_ring("c", (3, 0))
-    inp.finish_ring("a", (1, 2, 3, 0))
-    inp.sum_second()
-    inp.sum_third(in_ref)
-    for group in sent[32 - SLOTS :]:
-        for copy in group:
-            copy.wait_send()
+            wait_gate_up()
+        turn("bc", n - first_bc)
+        produce("bc", n - first_bc + 2)
+        turn("a", n - first_a)
+        produce("a", n - first_a + 2)
+        for which, start in ((out, 0), (inp, 16)):
+            k = n - first_bc - start
+            if k == 17:
+                which.sum_second("b")
+            if k == 18:
+                which.sum_second("c")
+        if n == first_a + 18:
+            out.sum_second("a")
+        if n == first_a + 22:
+            for part in PARTS:
+                out.sum_third(part, out_ref)
+    inp.sum_second("a")
+    for part in PARTS:
+        inp.sum_third(part, in_ref)
+    for kind in ("a", "bc"):
+        for group in sent[kind][32 - SLOTS :]:
+            for copy in group:
+                copy.wait_send()
     copies.drain()
     back.drain()
     dgrad.wait()

time: 185 us -> 178 us (0.962)
  Pallas kernels: 175 us -> 168 us
    pallas_call x1, Pallas kernels: 175 us -> 168 us  [per_device(): pl.pallas_call(moe_kernel, name='moe', out_shape=(jax.ShapeDtypeStruct((1...]
where the time goes in v4:
time: 178 us
  Pallas kernels  168 us (94%)
  local copies, waits for them, and re-layouts  7.48 us (4%)
    pallas_call x1, Pallas kernels, per_device(): pl.pallas_call(moe_kernel, name='moe', out_shape=(jax.ShapeDtypeStruct((1...  168 us
    unnamed x3, local copies, waits for them, and re-layouts  6.72 us

profile of v4, /device:TPU:8, one launch (start us, length us, event | category | flops | bytes accessed | tf_op | source)
XLA Modules:
  0.0 178.1 jit_solution(5293802133774217435)
XLA Ops:
  0.6 0.8 slice_bitcast_fusion.1
  1.4 0.8 broadcast_subtract_fusion
  2.2 0.7 select_select_fusion.meta_ref
  2.9 168.5 %moe.1 = (bf16[192,128]{1,0:T(8,128)(2,1)}, bf16[192,128]{1,0:T(8,128)(2,1)}, bf16[256,6144]{1,0:T(8,128)(2,1)}) custom-call(f32[8,8,128]{2,1,0:T(8,128)} %select_select_fusion.meta_ref, bf16[192,128]{1,0:T(8,128)(2,1)} %bitcast.19, bf16[192,128]{1,0:T(8,128)(2,1)} %bitcast.20, bf16[8,4,3,64,256]{4,3,2,1,0:T(8,128)(2,1)} %bitcast.16, ...), custom_call_target="tpu_custom_call" | custom-call | tf_op jit(solution)/shard_map/moe/pallas_call | solution.py:831
  171.3 1.4 copy.14
  172.8 1.4 copy.15
  174.2 3.9 %copy.16 = bf16[1,256,6144]{2,1,0:T(8,128)(2,1)} copy(bf16[1,256,6144]{2,1,0:T(8,128)(2,1)} %bitcast.15) | data formatting | bytes 6291456
  (2 shorter events, 0.0 us)

commit v5 on v4

--- a/solution.py
+++ b/solution.py
@@ -29,20 +29,45 @@
         self.seg = seg
         self.y, self.c = seg // 2, seg % 2
         self.z, self.x = fsdp // NX, fsdp % NX
+        self.other = 1 - self.c
+        self.xs = [self.x] + [lax.rem(self.x + d, NX) for d in range(1, NX)]
+        self.ys = [self.y] + [lax.rem(self.y + d, NY) for d in range(1, NY)]
+        self.zs = [self.z] + [lax.rem(self.z + d, NZ) for d in range(1, NZ)]
+        self.segs = [seg] + [lax.rem(seg + d, 8) for d in range(1, 8)]
+        self.za = [z * 4 for z in self.zs]
+        self.xb = [32 + x * 8 for x in self.xs]
+        self.yc = [64 + y * 8 for y in self.ys]
+        self.y2 = [y * 2 for y in self.ys]
+        self.x2 = [x * 2 for x in self.xs]
+        self.half = [z // 4 for z in self.zs]
+        self.low = [mult(lax.rem(z, 4) * FEAT, FEAT) for z in self.zs]
+        self.quarter = [lax.rem(z, 4) for z in self.zs]
+        self.known = {}
 
     def at(self, dx=0, dy=0, dz=0, sibling=False):
-        x = (self.x + dx) % NX
-        y = (self.y + dy) % NY
-        z = (self.z + dz) % NZ
-        c = 1 - self.c if sibling else self.c
-        return (y * 2 + c, z * NX + x)
-
-    def others(self):
-        found = [self.at(sibling=True)]
-        found += [self.at(dx=d) for d in range(1, NX)]
-        found += [self.at(dy=d) for d in range(1, NY)]
-        found += [self.at(dz=d) for d in range(1, NZ)]
-        return found
+        key = (dx % NX, dy % NY, dz % NZ, sibling)
+        if key not in self.known:
+            dx, dy, dz, _ = key
+            c = self.other if sibling else self.c
+            self.known[key] = (self.ys[dy] * 2 + c, self.zs[dz] * NX + self.xs[dx])
+        return self.known[key]
+
+    def brick(self, part, ahead, rel):
+        if part == "a":
+            return self.za[ahead % NZ] + self.ys[rel % NY]
+        if part == "b":
+            return self.xb[ahead % NX] + self.y2[rel % NY]
+        return self.yc[ahead % NY] + self.x2[rel % NX]
+
+    def weight(self, part, ahead, rel):
+        if part == "a":
+            return self.zs[ahead % NZ]
+        if part == "b":
+            return 8 + self.x2[ahead % NX]
+        return 16 + self.x2[rel % NX]
+
+    def row(self, part, ahead, rel):
+        return self.ys[(ahead if part == "c" else rel) % NY]
 
 
 def enter(devices):
@@ -72,16 +97,6 @@
         return [(4, r) for r in last] + [(h, r) for h in (3, 2, 1) for r in rows]
     rows, last = ((1, 2, 3, 0), (2, 0)) if sign > 0 else ((2, 1, 3, 0), (1, 3))
     return [(2, r) for r in last] + [(1, r) for r in rows]
-
-
-def weight_of(b):
-    in_b = 8 + ((b - 32) // 8) * 2 + b % 2
-    in_c = 16 + (((b - 64) // 2) % 4) * 2 + b % 2
-    return jnp.where(b < 32, b // 4, jnp.where(b < 64, in_b, in_c))
-
-
-def row_of(b):
-    return jnp.where(b < 32, b % 4, jnp.where(b < 64, ((b - 32) // 2) % 4, (b - 64) // 8))
 
 
 def mult(value, of):
@@ -135,25 +150,23 @@
     def key(self, *rest):
         return (self.name,) + rest
 
-    def atoms(self, x, z):
-        p = self.at
-        low = mult((z % 4) * FEAT, FEAT)
+    def atoms(self, dx, dz):
+        p = self.at
+        own = mult(p.xs[dx % NX] * FEAT, FEAT)
+        half, low = p.half[dz % NZ], p.low[dz % NZ]
         return (
-            self.buf.at[p.c, z * 4 + p.y, pl.ds(mult(x * FEAT, FEAT), FEAT)],
-            self.buf.at[p.c, 32 + (x * 4 + p.y) * 2 + z // 4, pl.ds(low, FEAT)],
-            self.buf.at[p.c, 64 + (p.y * 4 + x) * 2 + z // 4, pl.ds(low, FEAT)],
+            self.buf.at[p.c, p.za[dz % NZ] + p.y, pl.ds(own, FEAT)],
+            self.buf.at[p.c, p.xb[dx % NX] + p.y2[0] + half, pl.ds(low, FEAT)],
+            self.buf.at[p.c, p.yc[0] + p.x2[dx % NX] + half, pl.ds(low, FEAT)],
         )
 
     def put_own(self, block_t):
-        p = self.at
-        low = mult((p.z % 4) * FEAT, FEAT)
-        self.buf[p.c, p.z * 4 + p.y, pl.ds(mult(p.x * FEAT, FEAT), FEAT), :] = block_t[0:64]
-        self.buf[p.c, 32 + (p.x * 4 + p.y) * 2 + p.z // 4, pl.ds(low, FEAT), :] = block_t[64:128]
-        self.buf[p.c, 64 + (p.y * 4 + p.x) * 2 + p.z // 4, pl.ds(low, FEAT), :] = block_t[128:192]
+        for k, ref in enumerate(self.atoms(0, 0)):
+            ref[...] = block_t[k * FEAT : (k + 1) * FEAT]
 
     def send_first(self):
         p = self.at
-        a, b, c = self.atoms(p.x, p.z)
+        a, b, c = self.atoms(0, 0)
         for d in range(1, NX):
             self.copies.start(self.key("a1", d), a, a, p.at(dx=d))
         for d in range(1, NZ):
@@ -163,23 +176,20 @@
     def wait_first_a(self):
         p = self.at
         for d in range(1, NX):
-            a, _, _ = self.atoms((p.x - d) % NX, p.z)
+            a, _, _ = self.atoms(-d, 0)
             self.copies.arrived(self.key("a1", d), a, p.at(dx=-d))
 
     def wait_first_bc(self):
         p = self.at
         for d in range(1, NZ):
-            _, b, c = self.atoms(p.x, (p.z - d) % NZ)
+            _, b, c = self.atoms(0, -d)
             self.copies.arrived(self.key("b1", d), b, p.at(dz=-d))
             self.copies.arrived(self.key("c1", d), c, p.at(dz=-d))
 
     def second(self, part, rel):
         p = self.at
-        if part == "a":
-            return self.buf.at[p.c, p.z * 4 + (p.y + rel) % NY]
-        if part == "b":
-            return self.buf.at[p.c, pl.ds(32 + (p.x * 4 + (p.y + rel) % NY) * 2, 2)]
-        return self.buf.at[p.c, pl.ds(64 + (p.y * 4 + (p.x + rel) % NX) * 2, 2)]
+        base = p.brick(part, 0, rel)
+        return self.buf.at[p.c, base] if part == "a" else self.buf.at[p.c, pl.ds(base, 2)]
 
     def half(self, part, rel, sign):
         block = self.second(part, rel)
@@ -219,17 +229,12 @@
         return self.buf.at[self.at.c, pl.ds(base, SIZE[part])]
 
     def base(self, part, back, rel):
-        p = self.at
-        if part == "a":
-            return ((p.z - back) % NZ) * 4 + (p.y + rel) % NY
-        if part == "b":
-            return 32 + (((p.x - back) % NX) * 4 + (p.y + rel) % NY) * 2
-        return 64 + (((p.y - back) % NY) * 4 + (p.x + rel) % NX) * 2
+        return self.at.brick(part, -back, rel)
 
     def span(self, part, c):
         p = self.at
         first, count = {
-            "a": (p.z * 4, 4), "b": (32 + p.x * 8, 8), "c": (64 + p.y * 8, 8)
+            "a": (p.za[0], 4), "b": (p.xb[0], 8), "c": (p.yc[0], 8)
         }[part]
         return self.buf.at[c, pl.ds(first, count)]
 
@@ -263,48 +268,54 @@
     def wait_other(self, s, u):
         p = self.at
         for part, sign, hop, rel in self.messages(s, u):
-            ref = self.buf.at[1 - p.c, pl.ds(self.base(part, sign * hop, rel), SIZE[part])]
+            ref = self.buf.at[p.other, pl.ds(self.base(part, sign * hop, rel), SIZE[part])]
             self.copies.arrived(self.key("sib", part, sign, hop, rel), ref, p.at(sibling=True))
 
     def wait_other_own(self):
         for part in ("a", "b", "c"):
             self.copies.arrived(
-                self.key("own", part), self.span(part, 1 - self.at.c), self.at.at(sibling=True)
+                self.key("own", part), self.span(part, self.at.other), self.at.at(sibling=True)
             )
 
     def both(self, b):
         return jnp.concatenate([self.buf[0, b], self.buf[1, b]], axis=1)
 
-    def multiply_single(self, weights, total, b):
-        total[b % 4] += dot(weights(b // 4), self.both(b))
-
-    def multiply_chunk(self, weights, total, b):
-        w = weight_of(b)
+    def multiply_single(self, weights, total, b, w, row):
+        total[row] += dot(weights(w), self.both(b))
+
+    def multiply_chunk(self, weights, total, b, w, row):
         rhs = jnp.concatenate([self.both(b), self.both(b + 1)], axis=0)
-        total[row_of(b)] += dot(jnp.concatenate([weights(w), weights(w + 1)], axis=1), rhs)
+        total[row] += dot(jnp.concatenate([weights(w), weights(w + 1)], axis=1), rhs)
 
     def multiply_own(self, weights, total):
         p = self.at
 
         def step(t, carry):
-            self.multiply_single(weights, total, p.z * 4 + t)
-            self.multiply_chunk(weights, total, 32 + p.x * 8 + 2 * t)
-            self.multiply_chunk(weights, total, 64 + p.y * 8 + 2 * t)
+            self.multiply_single(weights, total, p.za[0] + t, p.z, t)
+            self.multiply_chunk(weights, total, p.xb[0] + 2 * t, 8 + p.x2[0], t)
+            self.multiply_chunk(weights, total, p.yc[0] + 2 * t, 16 + 2 * t, p.y)
             return carry
 
         lax.fori_loop(0, 4, step, 0)
 
     def multiply_round(self, weights, total, s, u):
+        p = self.at
         messages = self.messages(s, u)
-        bases = [self.base(part, sign * hop, rel) for part, sign, hop, rel in messages]
-        if not bases:
+        if not messages:
             return
+        facts = [
+            [f(part, -sign * hop, rel) for f in (p.brick, p.weight, p.row)]
+            for part, sign, hop, rel in messages
+        ]
 
         def step(t, carry):
+            def of(i):
+                return [jnp.where(t == 0, u, v) for u, v in zip(facts[i], facts[i + 1])]
+
             if messages[0][0] == "a":
-                self.multiply_single(weights, total, jnp.where(t == 0, bases[0], bases[1]))
+                self.multiply_single(weights, total, *of(0))
             if messages[-1][0] != "a":
-                self.multiply_chunk(weights, total, jnp.where(t == 0, bases[-2], bases[-1]))
+                self.multiply_chunk(weights, total, *of(len(facts) - 2))
             return carry
 
         lax.fori_loop(0, 2, step, 0)
@@ -334,12 +345,7 @@
         return (self.name,) + rest
 
     def base(self, part, ahead, rel):
-        p = self.at
-        if part == "a":
-            return ((p.z + ahead) % NZ) * 4 + (p.y + rel) % NY
-        if part == "b":
-            return 32 + (((p.x + ahead) % NX) * 4 + (p.y + rel) % NY) * 2
-        return 64 + (((p.y + ahead) % NY) * 4 + (p.x + rel) % NX) * 2
+        return self.at.brick(part, ahead, rel)
 
     def chunks(self, kind, j):
         part, n = ("a", j) if kind == "a" else (("b", "c")[j % 2], j // 2)
@@ -361,6 +367,10 @@
         slot = (self.first + j) % SLOTS
         chunks = self.chunks(kind, j)
         bases = [self.base(part, sign * hop, rel) for part, sign, hop, rel in chunks]
+        facts = [
+            [f(part, sign * hop, rel) for f in (p.weight, p.row)]
+            for part, sign, hop, rel in chunks
+        ]
 
         def one(w, rhs, at):
             value = dot(self.lhs(w), rhs).astype(BF)
@@ -368,14 +378,14 @@
             self.stage[slot, at] = value[:, TOK:]
 
         def rhs_of(row):
-            return jnp.concatenate([self.rhs(row, p.c), self.rhs(row, 1 - p.c)], axis=1)
+            return jnp.concatenate([self.rhs(row, p.c), self.rhs(row, p.other)], axis=1)
 
         def step(t, carry):
-            b = jnp.where(t == 0, bases[0], bases[1])
+            w, row = [jnp.where(t == 0, u, v) for u, v in zip(*facts)]
+            rhs = rhs_of(row)
             if kind == "a":
-                one(b // 4, rhs_of(b % 4), t)
+                one(w, rhs, t)
             else:
-                w, rhs = weight_of(b), rhs_of(row_of(b))
                 one(w, rhs, 2 + 2 * t)
                 one(w + 1, rhs, 3 + 2 * t)
             return carry
@@ -444,11 +454,12 @@
 
     def second(self, part, d):
         p = self.at
+        base = p.brick(part, 0, d)
         if part == "a":
-            return pl.ds(p.z * 4 + (p.y + d) % NY, 1), pl.ds(0, 1), p.at(dy=d)
+            return pl.ds(base, 1), pl.ds(0, 1), p.at(dy=d)
         if part == "b":
-            return pl.ds(32 + (p.x * 4 + (p.y + d) % NY) * 2, 2), pl.ds(1, 2), p.at(dy=d)
-        return pl.ds(64 + (p.y * 4 + (p.x + d) % NX) * 2, 2), pl.ds(3, 2), p.at(dx=d)
+            return pl.ds(base, 2), pl.ds(1, 2), p.at(dy=d)
+        return pl.ds(base, 2), pl.ds(3, 2), p.at(dx=d)
 
     def sum_second(self, part):
         p = self.at
@@ -458,28 +469,22 @@
             device = p.at(dx=-d) if part == "c" else p.at(dy=-d)
             self.copies.arrived(self.key(part + "2", d), self.two.at[d - 1, slot], device)
         for t, slot in enumerate(slots):
-            mine = {
-                "a": p.z * 4 + p.y,
-                "b": 32 + (p.x * 4 + p.y) * 2 + t,
-                "c": 64 + (p.y * 4 + p.x) * 2 + t,
-            }[part]
+            mine = p.brick(part, 0, 0) + t
             value = self.pairs[mine].astype(F32)
             for d in range(3):
                 value += self.two[d, slot].astype(F32)
             self.sums[slot] = value.astype(BF).reshape(4, 64, TOK)
         if part == "a":
             for d in range(1, NX):
-                x = (p.x + d) % NX
                 self.copies.start(
-                    self.key("a3", d), self.sums.at[0, x], self.three_a.at[d - 1], p.at(dx=d)
+                    self.key("a3", d), self.sums.at[0, p.xs[d]], self.three_a.at[d - 1], p.at(dx=d)
                 )
             return
         first, i = {"b": (1, 0), "c": (3, 1)}[part]
         for d in range(1, NZ):
-            z = (p.z + d) % NZ
             self.copies.start(
                 self.key(part + "3", d),
-                self.sums.at[first + z // 4, z % 4],
+                self.sums.at[first + p.half[d], p.quarter[d]],
                 self.three_bc.at[i, d - 1],
                 p.at(dz=d),
             )
@@ -494,7 +499,7 @@
             out_ref[0:FEAT] = value.astype(BF)
             return
         first, i = {"b": (1, 0), "c": (3, 1)}[part]
-        value = self.sums[first + p.z // 4, p.z % 4].astype(F32)
+        value = self.sums[first + p.half[0], p.quarter[0]].astype(F32)
         for d in range(1, NZ):
             self.copies.arrived(self.key(part + "3", d), self.three_bc.at[i, d - 1], p.at(dz=-d))
             value += self.three_bc[i, d - 1].astype(F32)
@@ -502,7 +507,9 @@
 
 
 def moe_kernel(
-    meta_ref,
+    logits_ref,
+    routes_ref,
+    losses_ref,
     tok_ref,
     cot_ref,
     gate_hbm,
@@ -522,6 +529,7 @@
     scaled,
     hid,
     grads,
+    weighing,
     meta,
     ring_a,
     ring_bc,
@@ -544,7 +552,8 @@
     back = Copies(send2, recv2)
     tok = Gather("tok", p, copies, tok_buf)
     cot = Gather("cot", p, copies, cot_buf)
-    far = [((p.seg + d) % 8, p.z * NX + p.x) for d in range(1, 8)]
+    here = p.at()[1]
+    far = [(p.segs[d], here) for d in range(1, 8)]
     line = [p.at(dx=d) for d in range(1, NX)] + [p.at(dz=d) for d in range(1, NZ)]
     entered = enter(line + far)
 
@@ -560,14 +569,23 @@
 
     tok.put_own(tok_ref)
     cot.put_own(cot_ref)
-    meta[p.seg] = meta_ref[p.seg]
+    share = jax.nn.sigmoid(logits_ref[0:1] - logits_ref[1:2])
+    scale = losses_ref[...].astype(F32) / 4096.0
+    weighing[...] = jnp.zeros_like(weighing)
+    for e in range(8):
+        combine = jnp.where(routes_ref[0:1] == e, share, 0.0) + jnp.where(
+            routes_ref[1:2] == e, 1.0 - share, 0.0
+        )
+        weighing[e, 0:1] = combine
+        weighing[e, 1:2] = combine * scale
+    meta[p.seg] = weighing[p.seg]
     total[...] = jnp.zeros_like(total)
     hgrad[...] = jnp.zeros_like(hgrad)
     entered()
 
     tok.send_first()
     for d in range(1, 8):
-        copies.start(("meta", d), meta_ref.at[(p.seg + d) % 8], meta.at[p.seg], far[d - 1])
+        copies.start(("meta", d), weighing.at[p.segs[d]], meta.at[p.seg], far[d - 1])
 
     def turn_gu(w, carry):
         for k in range(2):
@@ -703,7 +721,7 @@
     tok.second_far("a")
     lax.fori_loop(8, 16, turn_gu, 0)
 
-    lag, first_bc, first_a = 4, 23, 27
+    lag, first_bc, first_a = 3, 23, 27
     for n in range(first_a + 32):
         if n < 14:
             tok.ring_round(n, -1)
@@ -727,8 +745,8 @@
         if n == 4:
             tok.wait_other_own()
             tok.multiply_own(w_gu, total)
-        if 1 <= n <= 16:
-            k = n - 1
+        if 2 <= n <= 17:
+            k = n - 2
             tok.wait_other(k, k - lag)
             tok.multiply_round(w_gu, total, k, k - lag)
         if 5 <= n < 9:
@@ -753,17 +771,17 @@
         if n == 12:
             cot.second_far("b")
             cot.second_far("c")
-        if n == 16:
+        if n == 17:
             before, copies.sent = copies.sent, []
             load_gate_up()
             for d in range(1, 8):
-                copies.arrived(("meta", d), meta.at[(p.seg - d) % 8], far[7 - d])
+                copies.arrived(("meta", d), meta.at[p.segs[8 - d]], far[7 - d])
             lax.fori_loop(0, 16, activate, 0)
         if n == 17:
             cot.wait_other_own()
             cot.multiply_own(w_down, hgrad)
-        if 15 <= n <= 28:
-            k = n - 1
+        if 16 <= n <= 29:
+            k = n - 2
             cot.wait_other(k - 14, k - 12 - lag)
             cot.multiply_round(w_down, hgrad, k - 14, k - 12 - lag)
         if n == 20:
@@ -774,7 +792,7 @@
             )
         if n == 21:
             pl.semaphore_wait(free, 1)
-        if n == 28:
+        if n == 29:
             lax.fori_loop(0, 16, backward, 0)
         if 29 <= n < 37:
             lax.fori_loop(2 * n - 58, 2 * n - 56, weight_grad, 0)
@@ -812,15 +830,6 @@
 def per_device(
     tokens, router_logits, routes, loss_weights, cotangent, gate_weight, up_weight, down_weight
 ):
-    share = jax.nn.sigmoid(router_logits[:, 0] - router_logits[:, 1])
-    experts = jnp.arange(8, dtype=jnp.int32)[:, None]
-    combine = jnp.where(routes[None, :, 0] == experts, share[None, :], 0.0) + jnp.where(
-        routes[None, :, 1] == experts, 1.0 - share[None, :], 0.0
-    )
-    scale = combine * (loss_weights.astype(F32) / 4096.0)[None, :]
-    row = jnp.arange(8)[None, :, None]
-    meta = jnp.where(row == 0, combine[:, None, :], jnp.where(row == 1, scale[:, None, :], 0.0))
-
     gate5 = gate_weight.reshape(NZ, NX, 3, FEAT, 256)
     up5 = up_weight.reshape(NZ, NX, 3, FEAT, 256)
     down2 = down_weight.reshape(256, 6144)
@@ -836,7 +845,7 @@
             jax.ShapeDtypeStruct((192, TOK), BF),
             jax.ShapeDtypeStruct((256, 6144), BF),
         ),
-        in_specs=[vmem, vmem, vmem, hbm, hbm, hbm],
+        in_specs=[vmem] * 5 + [hbm] * 3,
         out_specs=(vmem, vmem, hbm),
         scratch_shapes=[
             pltpu.VMEM((2, 96, 256, TOK), BF),
@@ -850,6 +859,7 @@
             pltpu.VMEM((NY, 256, 256), BF),
             pltpu.VMEM((NY, 2, 256, TOK), BF),
             pltpu.VMEM((NY, 2, 512, TOK), BF),
+            pltpu.VMEM((8, 8, TOK), F32),
             pltpu.VMEM((8, 8, TOK), F32),
             pltpu.VMEM((2, 2, 14, 256, TOK), BF),
             pltpu.VMEM((2, 2, 2, 12, 256, TOK), BF),
@@ -870,7 +880,16 @@
         compiler_params=pltpu.CompilerParams(
             collective_id=1, has_side_effects=True, vmem_limit_bytes=62 * 2**20
         ),
-    )(meta, tokens.T, cotangent.T, gate5, up5, down2)
+    )(
+        router_logits.T,
+        routes.T,
+        loss_weights.reshape(1, TOK),
+        tokens.T,
+        cotangent.T,
+        gate5,
+        up5,
+        down2,
+    )
     return (output.T, input_grad.T, dgrad.reshape(1, 256, 6144))
 
 

time: 178 us -> 168 us (0.944); the launches traced: 178 us -> 166 us
  Pallas kernels: 168 us -> 158 us
    pallas_call x1, Pallas kernels: 168 us -> 158 us  [per_device(): pl.pallas_call(moe_kernel, name='moe', out_shape=(jax.ShapeDtypeStruct((1...]
where the time goes in v5:
time: 168 us; the launch traced here: 166 us
  Pallas kernels  158 us (94%)
  local copies, waits for them, and re-layouts  6.72 us (4%)
    pallas_call x1, Pallas kernels, per_device(): pl.pallas_call(moe_kernel, name='moe', out_shape=(jax.ShapeDtypeStruct((1...  158 us
    unnamed x3, local copies, waits for them, and re-layouts  6.72 us

profile of v5, /device:TPU:8, one launch (start us, length us, event | category | flops | bytes accessed | tf_op | source)
XLA Modules:
  0.0 165.8 jit_solution(2611582686567566981)
XLA Ops:
  0.6 158.4 %moe.1 = (bf16[192,128]{1,0:T(8,128)(2,1)}, bf16[192,128]{1,0:T(8,128)(2,1)}, bf16[256,6144]{1,0:T(8,128)(2,1)}) custom-call(f32[2,128]{1,0:T(2,128)} %bitcast.19, s32[2,128]{1,0:T(2,128)} %bitcast.20, s32[1,128]{1,0:T(1,128)} %bitcast.21, bf16[192,128]{1,0:T(8,128)(2,1)} %bitcast.15, bf16[192,128]{1,0:T(8,128)(2,1)} %bitcast.16, ...), custom_call_target="tpu_custom_call" | custom-call | tf_op jit(solution)/shard_map/moe/pallas_call | solution.py:840
  159.0 1.4 copy.14
  160.5 1.4 copy.15
  161.9 3.9 %copy.16 = bf16[1,256,6144]{2,1,0:T(8,128)(2,1)} copy(bf16[1,256,6144]{2,1,0:T(8,128)(2,1)} %bitcast.11) | data formatting | bytes 6291456

commit v6 on v5

--- a/solution.py
+++ b/solution.py
@@ -784,13 +784,13 @@
             k = n - 2
             cot.wait_other(k - 14, k - 12 - lag)
             cot.multiply_round(w_down, hgrad, k - 14, k - 12 - lag)
-        if n == 20:
+        if n == 19:
             for copy in before:
                 copy.wait_send()
             pl.semaphore_signal(
                 free, inc=1, device_id=p.at(sibling=True), device_id_type=MESH
             )
-        if n == 21:
+        if n == 20:
             pl.semaphore_wait(free, 1)
         if n == 29:
             lax.fori_loop(0, 16, backward, 0)
@@ -799,11 +799,12 @@
         if n == 37:
             dgrad = pltpu.make_async_copy(flat, dgrad_hbm, osem)
             dgrad.start()
+        if n == 36:
             wait_gate_up()
         turn("bc", n - first_bc)
-        produce("bc", n - first_bc + 2)
+        produce("bc", n - first_bc + 3)
         turn("a", n - first_a)
-        produce("a", n - first_a + 2)
+        produce("a", n - first_a + 3)
         for which, start in ((out, 0), (inp, 16)):
             k = n - first_bc - start
             if k == 17:
@@ -825,6 +826,22 @@
     copies.drain()
     back.drain()
     dgrad.wait()
+
+
+def hand_out_kernel(out_in, in_in, grad_in, out_ref, in_ref, grad_ref, sems):
+    copies = [
+        pltpu.make_async_copy(out_in, out_ref, sems.at[0]),
+        pltpu.make_async_copy(in_in, in_ref, sems.at[1]),
+    ]
+    for k in range(8):
+        rows = pl.ds(32 * k, 32)
+        copies.append(
+            pltpu.make_async_copy(grad_in.at[rows], grad_ref.at[rows], sems.at[2 + k])
+        )
+    for copy in copies:
+        copy.start()
+    for copy in copies:
+        copy.wait()
 
 
 def per_device(
@@ -890,6 +907,18 @@
         up5,
         down2,
     )
+    output, input_grad, dgrad = pl.pallas_call(
+        hand_out_kernel,
+        name="hand_out",
+        out_shape=(
+            jax.ShapeDtypeStruct((192, TOK), BF),
+            jax.ShapeDtypeStruct((192, TOK), BF),
+            jax.ShapeDtypeStruct((256, 6144), BF),
+        ),
+        in_specs=[hbm] * 3,
+        out_specs=(hbm,) * 3,
+        scratch_shapes=[pltpu.SemaphoreType.DMA((10,))],
+    )(output, input_grad, dgrad)
     return (output.T, input_grad.T, dgrad.reshape(1, 256, 6144))
 
 

time: 168 us -> 261 us (1.55)
  Pallas kernels: 158 us -> 259 us
  local copies, waits for them, and re-layouts: 6.72 us -> 0 us
    pallas_call x0 -> x1, Pallas kernels: none -> 99.5 us  [per_device(): pl.pallas_call(hand_out_kernel, name='hand_out', out_shape=(jax.ShapeDtyp...]
    unnamed x3 -> x0, local copies, waits for them, and re-layouts: 6.72 us -> none
where the time goes in v6:
time: 261 us; the launch traced here: 260 us
  Pallas kernels  259 us (99%)
    pallas_call x1, Pallas kernels, per_device(): pl.pallas_call(moe_kernel, name='moe', out_shape=(jax.ShapeDtypeStruct((1...  160 us
    pallas_call x1, Pallas kernels, per_device(): pl.pallas_call(hand_out_kernel, name='hand_out', out_shape=(jax.ShapeDtyp...  99.5 us

profile of v6, /device:TPU:8, one launch (start us, length us, event | category | flops | bytes accessed | tf_op | source)
XLA Modules:
  0.0 260.0 jit_solution(7972987300301241180)
XLA Ops:
  0.6 159.7 %moe.1 = (bf16[192,128]{1,0:T(8,128)(2,1)}, bf16[192,128]{1,0:T(8,128)(2,1)}, bf16[256,6144]{1,0:T(8,128)(2,1)}) custom-call(f32[2,128]{1,0:T(2,128)} %bitcast.16, s32[2,128]{1,0:T(2,128)} %bitcast.17, s32[1,128]{1,0:T(1,128)} %bitcast.18, bf16[192,128]{1,0:T(8,128)(2,1)} %bitcast.14, bf16[192,128]{1,0:T(8,128)(2,1)} %bitcast.15, ...), custom_call_target="tpu_custom_call" | custom-call | tf_op jit(solution)/shard_map/moe/pallas_call | solution.py:857
  160.4 99.5 %hand_out.1 = (bf16[192,128]{1,0:T(8,128)(2,1)}, bf16[192,128]{1,0:T(8,128)(2,1)}, bf16[256,6144]{1,0:T(8,128)(2,1)}) custom-call(bf16[192,128]{1,0:T(8,128)(2,1)} %get-tuple-element.9.out_in, bf16[192,128]{1,0:T(8,128)(2,1)} %get-tuple-element.10.in_in, bf16[256,6144]{1,0:T(8,128)(2,1)} %get-tuple-element.11.grad_in), custom_call_target="tpu_custom_call" | custom-call | tf_op jit(solution)/shard_map/hand_out/pallas_call | solution.py:910
